TPU v7x, 512 devices: a whole 4x8x8 slice. The times are simulated.
512 devices in a mesh: fsdp: 128 (over z, y, core), rep: 4 (over x).
Axes of the slice: x: 4, y: 8, z: 8, core: 2. Of those that a mesh axis runs over, the one named last changes fastest.
Arguments:
- grads: float32 [4, 128, 72, 4, 1024], P('rep', 'fsdp'), may hold values from -4 to 4
- momentum: float32 [128, 72, 4, 1024], P('fsdp'), may hold values from -6 to 6
- lengths: int32 [72, 128], replicated, may hold values from 1 to 4, 384 in all within a row
- owner: int32 [72], replicated, may hold values from 0 to 127, as said below
Outputs:
- new_momentum: float32 [128, 72, 4, 1024], P('fsdp')
- update: bfloat16 [128, 72, 4, 1024], P('fsdp')
- owned: bfloat16 [128, 384, 1024], P('fsdp')
Inputs may be any that keep to these rules, and one draw needn't show every extreme that they name: Row m of lengths adds up to 384, and one of its entries is exactly 4. `owner`: the owners of different matrices are different devices.
All inputs are finite; a program needn't handle non-finite values.
Results may differ from a plain program's by a relative error of at most 0.035.
Values may be sent and summed in bfloat16 or wider, within the bound.
No kernel may reach another device: no remote copies, remote signals or barrier semaphores. Data moves between devices by JAX's collectives and lax.ppermute only.
A program may use at most 64 MiB of HBM per device.

v0:
```python
import math

import jax
import jax.numpy as jnp
from jax import lax
from jax.sharding import PartitionSpec as P

R = 384
ITERS = 5


COEF_A = 3.4445
COEF_B = -4.775
COEF_C = 2.0315


def body(grads, momentum, lengths, owner):
    device_index = lax.axis_index("fsdp")
    fsdp_count = lax.axis_size("fsdp")
    count_mat = grads.shape[2]
    slot_count = grads.shape[3]
    width = grads.shape[4]
    rows_total = R
    total = lax.psum(grads[0, 0], "rep")
    lens_here = lax.dynamic_slice_in_dim(lengths, device_index, 1, 1)[:, 0]
    slot_ids = jnp.arange(slot_count, dtype=jnp.int32)
    live = slot_ids[None, :] < lens_here[:, None]
    new_momentum = jnp.where(live[..., None], 0.95 * momentum[0] + total, jnp.float32(0.0))
    matrix_ids = jnp.arange(count_mat, dtype=jnp.int32)
    is_mine = owner == device_index
    has_matrix = jnp.any(is_mine)
    my_matrix = jnp.sum(jnp.where(is_mine, matrix_ids, 0))
    lens_owned = lax.dynamic_slice_in_dim(lengths, my_matrix, 1, 0)[0]
    inclusive = jnp.cumsum(lens_owned)
    starts = inclusive - lens_owned
    row_ids = jnp.arange(rows_total, dtype=jnp.int32)
    source = jnp.sum((inclusive[None, :] <= row_ids[:, None]).astype(jnp.int32), axis=1)
    picked = source * slot_count + row_ids - starts[source]
    outgoing = jnp.zeros((fsdp_count, slot_count, width), jnp.float32).at[owner].set(new_momentum)
    incoming = lax.all_to_all(outgoing, "fsdp", split_axis=0, concat_axis=0, tiled=True)
    matrix = incoming.reshape(fsdp_count * slot_count, width)[picked]
    norm_value = jnp.sqrt(jnp.sum(matrix * matrix))
    iterate = (matrix / (norm_value + 1e-07)).astype(jnp.bfloat16)
    for step_index in range(ITERS):
        gram = jnp.dot(iterate, iterate.T, preferred_element_type=jnp.float32).astype(jnp.bfloat16)
        square = jnp.dot(gram, gram, preferred_element_type=jnp.float32)
        poly = (COEF_B * gram.astype(jnp.float32) + COEF_C * square).astype(jnp.bfloat16)
        iterate = (
            COEF_A * iterate.astype(jnp.float32)
            + jnp.dot(poly, iterate, preferred_element_type=jnp.float32)
        ).astype(jnp.bfloat16)
    scale = math.sqrt(max(rows_total, width))
    row_index = jnp.clip(starts[:, None] + slot_ids[None, :], 0, rows_total - 1)
    live_out = jnp.logical_and(slot_ids[None, :] < lens_owned[:, None], has_matrix)
    returning = jnp.where(live_out[..., None], iterate[row_index], jnp.bfloat16(0.0))
    arrived = lax.all_to_all(returning, "fsdp", split_axis=0, concat_axis=0, tiled=True)
    pieces = arrived[owner]
    update = jnp.where(
        live[..., None], -scale * pieces.astype(jnp.float32), jnp.float32(0.0)
    ).astype(jnp.bfloat16)
    owned = jnp.where(has_matrix, -scale * iterate.astype(jnp.float32), jnp.float32(0.0)).astype(
        jnp.bfloat16
    )
    return (new_momentum[None], update[None], owned[None])


def solution(mesh):
    in_specs = (P("rep", "fsdp", None, None, None), P("fsdp", None, None, None), P(), P())
    out_specs = (P("fsdp", None, None, None), P("fsdp", None, None, None), P("fsdp", None, None))
    return jax.shard_map(body, mesh=mesh, in_specs=in_specs, out_specs=out_specs, check_vma=False)
```

profile of v0, /device:TPU:1, one launch (start us, length us, event | category | flops | bytes accessed | tf_op | source)
XLA Modules:
  0.0 220.3 jit_solution(7742837921881868605)
XLA Ops:
  7.2 0.0 copy-start.2
  7.2 0.0 all-reduce.2.cloned.1.call-start
  7.2 0.7 all-reduce.2.cloned.1.call-update
  7.9 0.9 dynamic-slice_reduce_fusion
  8.9 1.3 fusion.36
  10.2 0.1 iota_compare_fusion.2
  10.3 61.7 %all-reduce.2.cloned.1.call-done = f32[72,4,1024]{2,1,0:T(4,128)} async-done(((f32[72,4,1024]{2,1,0:T(4,128)}), f32[72,4,1024]{2,1,0:T(4,128)}) %all-reduce.2.cloned.1.call-update) | async-done | bytes 1179664 | tf_op jit(solution)/shard_map/psum | solution.py:24
  72.0 0.0 copy-done.2
  72.0 1.8 fusion.11
  73.8 0.0 copy-start.1
  73.8 1.8 broadcast_in_dim.72
  75.6 10.1 %scatter_fusion = f32[128,4,1024]{2,1,0:T(4,128)} fusion(f32[128,4,1024]{2,1,0:T(4,128)} %broadcast_in_dim.72, s32[72]{0:T(128)S(1)} %get-tuple-element.6, f32[72,4,1024]{2,1,0:T(4,128)S(1)} %fusion.11), kind=kCustom, calls=%fused_computation.4 | custom fusion | bytes 3539232 | tf_op jit(solution)/shard_map/scatter | solution.py:39
  85.7 0.0 copy-done.1
  85.7 15.9 %all-to-all-start = ((f32[128,4,1024]{2,1,0:T(4,128)}), f32[128,4,1024]{2,1,0:T(4,128)}, u32[]{:S(2)}, u32[]{:S(2)}) async-start(f32[128,4,1024]{2,1,0:T(4,128)} %scatter_fusion), calls=%async_computation | async-start | bytes 4194304 | tf_op jit(solution)/shard_map/all_to_all | solution.py:40
  101.5 0.0 copy-start.3
  103.5 0.7 fusion.37
  104.2 0.1 copy.9
  104.3 0.2 reduce-window.7
  104.5 0.1 reduce.1
  104.6 0.2 convert_reduce_fusion
  104.8 0.7 fusion.49
  105.5 2.7 %gather_fusion = s32[384]{0:T(512)S(1)} fusion(s32[128]{0:T(128)S(1)} %get-tuple-element.3, s32[1024]{0:T(1024)S(1)} %pad_clamp_fusion.3), kind=kCustom, calls=%fused_computation | custom fusion | bytes 4608 | tf_op jit(solution)/shard_map/gather | solution.py:38
  108.2 0.1 compare_select_fusion
  108.3 0.1 reshape.209
  108.4 0.0 copy-done.3
  108.4 0.6 compare_reduce_fusion
  109.1 0.7 fusion.33
  109.8 42.7 %all-to-all-done = f32[128,4,1024]{2,1,0:T(4,128)} async-done(((f32[128,4,1024]{2,1,0:T(4,128)}), f32[128,4,1024]{2,1,0:T(4,128)}, u32[]{:S(2)}, u32[]{:S(2)}) %all-to-all-start) | async-done | bytes 2097184 | tf_op jit(solution)/shard_map/all_to_all | solution.py:40
  152.4 2.0 reshape.188
  154.4 2.5 %gather_fusion.1 = f32[384,1024]{1,0:T(8,128)} fusion(f32[512,1024]{1,0:T(8,128)S(1)} %reshape.188, s32[1024]{0:T(1024)S(1)} %pad_clamp_fusion.2), kind=kCustom, calls=%fused_computation.1 | custom fusion | bytes 3147264 | tf_op jit(solution)/shard_map/gather | solution.py:41
  156.9 0.0 copy-start
  156.9 2.5 %multiply_reduce_fusion = f32[]{:T(128)} fusion(f32[384,1024]{1,0:T(8,128)} %gather_fusion.1), kind=kLoop, calls=%fused_computation.12 | loop fusion | flops 786431 | bytes 1572868 | tf_op jit(solution)/shard_map/reduce_sum | solution.py:42
  160.2 0.0 copy-done
  160.2 0.6 convolution_convert_fusion.4
  160.8 0.8 add_convert_fusion.4
  161.6 0.6 convolution_convert_fusion.3
  162.2 0.8 add_convert_fusion.3
  163.1 0.6 convolution_convert_fusion.2
  163.6 0.8 add_convert_fusion.2
  164.5 0.6 convolution_convert_fusion.1
  165.1 0.8 add_convert_fusion.1
  165.9 0.6 convolution_convert_fusion
  166.5 0.8 add_convert_fusion
  167.3 2.1 gather_fusion.2
  169.4 0.4 reshape.208
  169.8 1.6 broadcast_select_fusion
  171.4 8.9 %all-to-all-start.1 = ((bf16[128,4,1024]{2,1,0:T(4,128)(2,1)}), bf16[128,4,1024]{2,1,0:T(4,128)(2,1)S(1)}, u32[]{:S(2)}, u32[]{:S(2)}) async-start(bf16[128,4,1024]{2,1,0:T(4,128)(2,1)} %broadcast_select_fusion), calls=%async_computation.1 | async-start | bytes 2097152 | tf_op jit(solution)/shard_map/all_to_all | solution.py:56
  180.4 1.7 fusion.12
  182.1 29.2 %all-to-all-done.1 = bf16[128,4,1024]{2,1,0:T(4,128)(2,1)S(1)} async-done(((bf16[128,4,1024]{2,1,0:T(4,128)(2,1)}), bf16[128,4,1024]{2,1,0:T(4,128)(2,1)S(1)}, u32[]{:S(2)}, u32[]{:S(2)}) %all-to-all-start.1) | async-done | bytes 1048608 | tf_op jit(solution)/shard_map/all_to_all | solution.py:56
  211.3 1.1 gather_fusion.3
  212.3 1.2 fusion.10
  (6 shorter events, 0.1 us)
Async XLA Ops:
  7.2 64.8 %copy-start.2 = (f32[1,72,4,1024]{3,2,1,0:T(4,128)S(1)}, f32[1,72,4,1024]{3,2,1,0:T(4,128)}, u32[]{:S(2)}) copy-start(f32[1,72,4,1024]{3,2,1,0:T(4,128)} %param.5) | copy-start | bytes 3538948
  7.2 64.8 %all-reduce.2.cloned.1.call-start = ((), (), s32[]{:S(2)}) async-start(), calls=%async_computation.2 | async-start | bytes 2359296 | tf_op jit(solution)/shard_map/psum | solution.py:24
  73.8 11.9 %copy-start.1 = (f32[72,4,1024]{2,1,0:T(4,128)}, f32[72,4,1024]{2,1,0:T(4,128)S(1)}, u32[]{:S(2)}) copy-start(f32[72,4,1024]{2,1,0:T(4,128)S(1)} %fusion.11) | copy-start | bytes 3538948
  85.7 66.8 %all-to-all-start = ((f32[128,4,1024]{2,1,0:T(4,128)}), f32[128,4,1024]{2,1,0:T(4,128)}, u32[]{:S(2)}, u32[]{:S(2)}) async-start(f32[128,4,1024]{2,1,0:T(4,128)} %scatter_fusion), calls=%async_computation | async-start | bytes 4194304 | tf_op jit(solution)/shard_map/all_to_all | solution.py:40
  101.5 6.9 %copy-start.3 = (s32[72]{0:T(128)S(1)}, s32[72]{0:T(128)}, u32[]{:S(2)}) copy-start(s32[72]{0:T(128)} %param.7) | copy-start | bytes 868
  156.9 3.2 %copy-start = (f32[384,1024]{1,0:T(8,128)S(1)}, f32[384,1024]{1,0:T(8,128)}, u32[]{:S(2)}) copy-start(f32[384,1024]{1,0:T(8,128)} %gather_fusion.1) | copy-start | bytes 4718596
  171.4 39.8 %all-to-all-start.1 = ((bf16[128,4,1024]{2,1,0:T(4,128)(2,1)}), bf16[128,4,1024]{2,1,0:T(4,128)(2,1)S(1)}, u32[]{:S(2)}, u32[]{:S(2)}) async-start(bf16[128,4,1024]{2,1,0:T(4,128)(2,1)} %broadcast_select_fusion), calls=%async_computation.1 | async-start | bytes 2097152 | tf_op jit(solution)/shard_map/all_to_all | solution.py:56
Sparse Core Ops, SparseCore 0:
  10.4 61.5 all-reduce.1
where the time goes:
time: 221 us; the launch traced here: 220 us
  waiting for transfers between devices  134 us (61%)
  starting transfers between devices  24.8 us (11%)
  local copies, waits for them, and re-layouts  24.5 us (11%)
  between operations  16.9 us (8%)
  other arithmetic  12.7 us (6%)
  matrix products  7.12 us (3%)
    psum x1, waiting for transfers between devices, body(): total = lax.psum(grads[0, 0], 'rep')  61.7 us
    all_to_all x1, waiting for transfers between devices, body(): lax.all_to_all(outgoing, 'fsdp', split_axis=0, concat_axis=0, tiled=True)  42.7 us
    all_to_all x1, waiting for transfers between devices, body(): lax.all_to_all(returning, 'fsdp', split_axis=0, concat_axis=0, tiled=True)  29.2 us
    all_to_all x1, starting transfers between devices, body(): lax.all_to_all(outgoing, 'fsdp', split_axis=0, concat_axis=0, tiled=True)  15.9 us
    scatter x1, local copies, waits for them, and re-layouts, body(): jnp.zeros((fsdp_count, slot_count, width), jnp.float32).at[owner]  10.1 us
    all_to_all x1, starting transfers between devices, body(): lax.all_to_all(returning, 'fsdp', split_axis=0, concat_axis=0, tiled=True)  8.93 us
  transfers between devices with their start and end apart: 3, of which 3 were waited for; matrix products, arithmetic and copies ran while one was open for 5% of the time, Pallas kernels for 0%

commit v1 on v0

v1 whole, which is shorter than its diff:
```python
import functools
import math

import jax
import jax.numpy as jnp
from jax import lax
from jax.experimental import pallas as pl
from jax.experimental.pallas import tpu as pltpu
from jax.sharding import PartitionSpec as P

R = 384
ITERS = 5

COEF_A = 3.4445
COEF_B = -4.775
COEF_C = 2.0315

LANES = 128
ROWS = 8
BF16 = jnp.bfloat16
F32 = jnp.float32
VMEM_LIMIT = 48 * 1024 * 1024


def vmem():
    return pl.BlockSpec(memory_space=pltpu.VMEM)


def hbm():
    return pl.BlockSpec(memory_space=pltpu.HBM)


def later():
    return pl.BlockSpec(memory_space=pl.ANY)


def smem():
    return pl.BlockSpec(memory_space=pltpu.SMEM)


def params(limit=VMEM_LIMIT):
    return pltpu.CompilerParams(vmem_limit_bytes=limit)


def cost(flops, nbytes):
    return pl.CostEstimate(flops=flops, bytes_accessed=nbytes, transcendentals=0)


def column_of(half, block):
    if isinstance(block, int):
        return block * 2 * LANES + half * LANES
    return pl.multiple_of(block * (2 * LANES) + half * LANES, LANES)


def to_rows(src_ref, block, scratch):
    slots = src_ref.shape[1]
    for half in range(2):
        scratch[:, half * slots:(half + 1) * slots, :] = src_ref[:, :, pl.ds(column_of(half, block), LANES)]
    return scratch[...].reshape(scratch.shape[0] * ROWS, LANES)


def split_kernel(g_ref, out_ref, arrived, scratch, packed, in_sems, out_sems):
    blocks = out_ref.shape[0]
    wide = 2 * LANES
    reads = [
        pltpu.make_async_copy(g_ref.at[:, :, block * wide:(block + 1) * wide], arrived.at[block], in_sems.at[block])
        for block in range(blocks)
    ]
    writes = [pltpu.make_async_copy(packed.at[block], out_ref.at[block], out_sems.at[block]) for block in range(blocks)]
    for read in reads:
        read.start()
    for block in range(blocks):
        reads[block].wait()
        packed[block] = to_rows(arrived.at[block], 0, scratch.at[block]).astype(BF16)
        writes[block].start()
    for write in writes:
        write.wait()


def own_kernel(owner_ref, lens_ref, mom_ref, base_ref, pick_ref, place_ref, scratch):
    base_ref[...] = 0.95 * to_rows(mom_ref, lax.axis_index("rep"), scratch)
    pick_kernel(owner_ref, lens_ref, pick_ref, place_ref)


def scatter_kernel(owner_ref, base_ref, parts_ref, send_ref, tot_ref, packed):
    reps = parts_ref.shape[0]
    total = parts_ref[0].astype(F32)
    for rep in range(1, reps):
        total = total + parts_ref[rep].astype(F32)
    tot_ref[...] = total.astype(BF16)
    nm = base_ref[...] + total
    packed[...] = jnp.zeros_like(packed)
    for m in range(nm.shape[0] // ROWS):
        at = pl.multiple_of(owner_ref[m] * ROWS, ROWS)
        packed[pl.ds(at, ROWS), :] = nm[m * ROWS:(m + 1) * ROWS, :]
    send_ref[...] = packed[...].astype(BF16)


def pick_kernel(owner_ref, lens_ref, pick_ref, place_ref):
    me = lax.axis_index("fsdp")
    rows, slots8 = pick_ref.shape
    count = lens_ref.shape[1]

    def find(m, found):
        return jnp.where(owner_ref[m] == me, m, found)

    mine = lax.fori_loop(0, lens_ref.shape[0], find, -1)
    lens = lens_ref[pl.ds(jnp.maximum(mine, 0), 1), :]
    lens = jnp.where(mine >= 0, lens, 0).astype(F32)
    many = jnp.broadcast_to(lens, (LANES, count)).astype(BF16)

    def table(shape, slot_dim, before):
        device = lax.broadcasted_iota(jnp.int32, shape, 1 - slot_dim)
        source = lax.broadcasted_iota(jnp.int32, shape, slot_dim) // ROWS
        hit = device < source if before else device == source
        return jnp.where(hit, F32(1.0), F32(0.0)).astype(BF16)

    def source_row(shape, slot_dim, start, length):
        slot = (lax.broadcasted_iota(jnp.int32, shape, slot_dim) % 4)
        return jnp.where(slot < length.astype(jnp.int32), start.astype(jnp.int32) + slot, -1)

    few = many[:16, :]
    start = jnp.dot(few, table((count, slots8), 1, True), preferred_element_type=F32)[:8]
    length = jnp.dot(few, table((count, slots8), 1, False), preferred_element_type=F32)[:8]
    source = source_row((8, slots8), 1, start, length)[:1]
    hit = lax.broadcasted_iota(jnp.int32, (rows, slots8), 0) == source
    pick_ref[...] = jnp.where(hit, F32(1.0), F32(0.0)).astype(BF16)

    contract = (((1,), (1,)), ((), ()))
    start = lax.dot_general(table((slots8, count), 0, True), many, contract, preferred_element_type=F32)
    length = lax.dot_general(table((slots8, count), 0, False), many, contract, preferred_element_type=F32)
    source = source_row((slots8, LANES), 0, start, length)
    for at in range(0, rows, LANES):
        some = min(LANES, rows - at)
        hit = lax.broadcasted_iota(jnp.int32, (slots8, some), 1) + at == source[:, :some]
        place_ref[:, at:at + some] = jnp.where(hit, F32(1.0), F32(0.0)).astype(BF16)


def in_half(shape, half):
    return (lax.broadcasted_iota(jnp.int32, shape, 0) // 4) % 2 == half


def compact_kernel(pick_ref, in_ref, _, out_ref):
    slots8 = pick_ref.shape[1]
    upper = in_half((slots8, LANES), 0)
    got = in_ref[...].astype(F32)
    both = jnp.concatenate([jnp.where(upper, got, 0.0), jnp.where(upper, 0.0, got)], axis=1).astype(BF16)
    picked = jnp.dot(pick_ref[...], both, preferred_element_type=F32).astype(BF16)
    for rep in range(out_ref.shape[0]):
        out_ref[rep] = picked


def newton_schulz_kernel(scale, place_ref, pieces_ref, total_ref, first_ref, owned_ref, back_ref, joined_ref, matrix, x):
    rows8 = total_ref.shape[0]
    joined_ref[:rows8, :] = total_ref[...]
    joined_ref[rows8:, :] = first_ref[...]
    me = lax.axis_index("rep")
    wide = 2 * LANES
    upper = in_half((place_ref.shape[0], LANES), 0)
    for block in range(pieces_ref.shape[0]):
        matrix[:, block * wide:(block + 1) * wide] = pieces_ref[block].astype(F32)
    squares = jnp.sum(matrix[...] * matrix[...])
    factor = 1.0 / (jnp.sqrt(jnp.full((1, LANES), squares, F32)) + 1e-07)
    for tile in range(matrix.shape[1] // LANES):
        at = slice(tile * LANES, (tile + 1) * LANES)
        x[:, at] = (matrix[:, at] * factor).astype(BF16)

    def step(index, carry):
        contract = (((1,), (1,)), ((), ()))
        gram = lax.dot_general(x[...], x[...], contract, preferred_element_type=F32).astype(BF16)
        square = jnp.dot(gram, gram, preferred_element_type=F32)
        poly = (COEF_B * gram.astype(F32) + COEF_C * square).astype(BF16)
        for tile in range(x.shape[1] // wide):
            at = slice(tile * wide, (tile + 1) * wide)
            part = x[:, at]
            x[:, at] = (COEF_A * part.astype(F32) + jnp.dot(poly, part, preferred_element_type=F32)).astype(BF16)
        return carry

    lax.fori_loop(0, ITERS, step, 0)
    owned_ref[...] = (-scale * x[...].astype(F32)).astype(BF16)
    mine = owned_ref[:, pl.ds(column_of(0, me), wide)]
    spread = jnp.dot(place_ref[...], mine, preferred_element_type=F32)
    back_ref[...] = jnp.where(upper, spread[:, :LANES], spread[:, LANES:]).astype(BF16)


def select_kernel(owner_ref, back_ref, _, out_ref, wide, chosen):
    wide[...] = back_ref[...].astype(F32)
    for m in range(chosen.shape[0] // ROWS):
        at = pl.multiple_of(owner_ref[m] * ROWS, ROWS)
        chosen[m * ROWS:(m + 1) * ROWS, :] = wide[pl.ds(at, ROWS), :]
    rounded = chosen[...].astype(BF16)
    for rep in range(out_ref.shape[0]):
        out_ref[rep] = rounded


def partners():
    core = lax.rem(lax.axis_index("fsdp"), 2)
    return 1 + 2 * core, 3 - 2 * core


def blocks_of(own_ref, first_ref, second_ref):
    me = lax.axis_index("rep")
    first, second = partners()
    rows = own_ref.shape[0]
    return (
        (me, own_ref),
        (me ^ first, first_ref),
        (me ^ second, second_ref.at[:rows]),
        (me ^ 2, second_ref.at[rows:]),
    )


def columns(blocks, count):
    slots = ROWS // 2
    for block, piece in blocks:
        got = piece[...].astype(F32).reshape(count, ROWS, LANES)
        for half in range(2):
            yield pl.ds(column_of(half, block), LANES), got[:, half * slots:(half + 1) * slots, :]


def update_kernel(pieces_ref, out_ref):
    for at, got in columns([(block, pieces_ref.at[block]) for block in range(pieces_ref.shape[0])], out_ref.shape[0]):
        out_ref[:, :, at] = got.astype(BF16)


def momentum_kernel(lens_ref, mom_ref, own_ref, first_ref, second_ref, out_ref, done_ref, total):
    done_ref[...] = jnp.zeros_like(done_ref)
    device = lax.axis_index("fsdp")
    count, slots, width = out_ref.shape
    for at, got in columns(blocks_of(own_ref, first_ref, second_ref), count):
        total[:, :, at] = got
    slot = lax.broadcasted_iota(jnp.int32, (slots, width), 0)
    for m in range(count):
        live = slot < lens_ref[m, device]
        out_ref[m] = jnp.where(live, 0.95 * mom_ref[m] + total[m], 0.0)


def swap(value, step):
    devices, reps = lax.axis_size("fsdp"), lax.axis_size("rep")
    pairs = []
    for device in range(devices):
        flip = (1, 3)[(device + step) % 2]
        pairs += [(device * reps + rep, device * reps + (rep ^ flip)) for rep in range(reps)]
    return lax.ppermute(value, ("fsdp", "rep"), pairs)


def exchange(value):
    flat = value.reshape((value.shape[0] * value.shape[1],) + value.shape[2:])
    return lax.all_to_all(flat, "rep", split_axis=0, concat_axis=0, tiled=True).reshape(value.shape)


def body(grads, momentum, lengths, owner):
    reps = lax.axis_size("rep")
    devices = lax.axis_size("fsdp")
    count, slots, width = momentum.shape[1:]
    g, mom = grads[0, 0], momentum[0]
    rows8, slots8 = count * ROWS, devices * ROWS
    shape = jax.ShapeDtypeStruct
    part = shape((rows8, LANES), BF16)
    parts = shape((reps, rows8, LANES), BF16)

    split = pl.pallas_call(
        split_kernel,
        out_shape=parts,
        in_specs=[hbm()],
        out_specs=hbm(),
        scratch_shapes=[
            pltpu.VMEM((reps, count, slots, 2 * LANES), F32),
            pltpu.VMEM((reps, count, ROWS, LANES), F32),
            pltpu.VMEM((reps, rows8, LANES), BF16),
            pltpu.SemaphoreType.DMA((reps,)),
            pltpu.SemaphoreType.DMA((reps,)),
        ],
        compiler_params=params(60 * 1024 * 1024),
        cost_estimate=cost(0, 2_000_000),
        name="split",
    )(g)
    got = exchange(split)
    base, pick, place = pl.pallas_call(
        own_kernel,
        out_shape=[shape((rows8, LANES), F32), shape((R, slots8), BF16), shape((slots8, R), BF16)],
        in_specs=[smem()] + [vmem()] * 2,
        out_specs=[vmem()] * 3,
        scratch_shapes=[pltpu.VMEM((count, ROWS, LANES), F32)],
        compiler_params=params(),
        cost_estimate=cost(0, 4_000_000),
        name="own",
    )(owner, lengths, mom)
    send, total = pl.pallas_call(
        scatter_kernel,
        out_shape=[shape((slots8, LANES), BF16), part],
        in_specs=[smem(), vmem(), vmem()],
        out_specs=[vmem()] * 2,
        scratch_shapes=[pltpu.VMEM((slots8, LANES), F32)],
        compiler_params=params(),
        cost_estimate=cost(0, 2_000_000),
        name="scatter",
    )(owner, base, got)
    first = swap(total, 0)
    incoming = lax.all_to_all(send, "fsdp", split_axis=0, concat_axis=0, tiled=True)
    compact = pl.pallas_call(
        compact_kernel,
        out_shape=shape((reps, R, 2 * LANES), BF16),
        in_specs=[vmem()] * 2 + [later()],
        out_specs=vmem(),
        compiler_params=params(),
        cost_estimate=cost(200_000_000, 2_000_000),
        name="compact",
    )(pick, incoming, first)

    pieces = exchange(compact)
    owned, back, joined = pl.pallas_call(
        functools.partial(newton_schulz_kernel, math.sqrt(max(R, width))),
        out_shape=[shape((R, width), BF16), shape((slots8, LANES), BF16), shape((2 * rows8, LANES), BF16)],
        in_specs=[vmem()] * 4,
        out_specs=[vmem()] * 3,
        scratch_shapes=[pltpu.VMEM((R, width), F32), pltpu.VMEM((R, width), BF16)],
        compiler_params=params(),
        cost_estimate=cost(5_000_000_000, 4_000_000),
        name="newton_schulz",
    )(place, pieces, total, first)
    returned = lax.all_to_all(back, "fsdp", split_axis=0, concat_axis=0, tiled=True)
    new_momentum, done = pl.pallas_call(
        momentum_kernel,
        out_shape=[shape((count, slots, width), F32), shape((8, LANES), F32)],
        in_specs=[smem()] + [vmem()] * 4,
        out_specs=[vmem()] * 2,
        scratch_shapes=[pltpu.VMEM((count, slots, width), F32)],
        compiler_params=params(),
        cost_estimate=cost(0, 4_000_000),
        name="momentum",
    )(lengths, mom, total, first, swap(joined, 1))
    chosen = pl.pallas_call(
        select_kernel,
        out_shape=parts,
        in_specs=[smem(), vmem(), later()],
        out_specs=vmem(),
        scratch_shapes=[pltpu.VMEM((slots8, LANES), F32), pltpu.VMEM((rows8, LANES), F32)],
        compiler_params=params(),
        cost_estimate=cost(0, 1_000_000),
        name="select",
    )(owner, returned, done)
    update = pl.pallas_call(
        update_kernel,
        out_shape=shape((count, slots, width), BF16),
        in_specs=[vmem()],
        out_specs=vmem(),
        compiler_params=params(),
        cost_estimate=cost(0, 2_000_000),
        name="update",
    )(exchange(chosen))
    return (new_momentum[None], update[None], owned[None])


def solution(mesh):
    in_specs = (P("rep", "fsdp", None, None, None), P("fsdp", None, None, None), P(), P())
    out_specs = (P("fsdp", None, None, None), P("fsdp", None, None, None), P("fsdp", None, None))
    return jax.shard_map(body, mesh=mesh, in_specs=in_specs, out_specs=out_specs, check_vma=False)
```

time: 221 us -> 112 us (0.51)
  waiting for transfers between devices: 134 us -> 26.9 us
  blocking collectives: 0 us -> 26.6 us
  local copies, waits for them, and re-layouts: 24.5 us -> 0.89 us
  Pallas kernels: 0 us -> 19.8 us
  between operations: 16.9 us -> 0.74 us
  other arithmetic: 12.7 us -> 0 us
  starting transfers between devices: 24.8 us -> 37 us
  matrix products: 7.12 us -> 0 us
    psum x1 -> x0, waiting for transfers between devices: 61.7 us -> none  [body(): total = lax.psum(grads[0, 0], 'rep')]
    all_to_all x2 -> x3, waiting for transfers between devices: 71.9 us -> 16.7 us  [the longest x1 7.86 us: body(): lax.all_to_all(send, 'fsdp', split_axis=0, concat_axis=0, tiled=True)]
    all_to_all x0 -> x2, blocking collectives: none -> 26.6 us  [exchange(): lax.all_to_all(flat, 'rep', split_axis=0, concat_axis=0, tiled=True)]
    pallas_call x0 -> x8, Pallas kernels: none -> 19.8 us  [the longest x1 9.12 us: body(): pl.pallas_call(functools.partial(newton_schulz_kernel, math.sqrt(max(R, w...]
    ppermute x0 -> x2, waiting for transfers between devices: none -> 10.1 us  [swap(): return lax.ppermute(value, ('fsdp', 'rep'), pairs)]
    scatter x1 -> x0, local copies, waits for them, and re-layouts: 10.1 us -> none  [body(): jnp.zeros((fsdp_count, slot_count, width), jnp.float32).at[owner]]
    gather x5 -> x0, local copies, waits for them, and re-layouts: 8.73 us -> none  [the longest x1 2.68 us: body(): picked = source * slot_count + row_ids - starts[source]]
    all_to_all x2 -> x3, starting transfers between devices: 24.8 us -> 32 us  [the longest x1 20.8 us: body(): lax.all_to_all(send, 'fsdp', split_axis=0, concat_axis=0, tiled=True)]
  transfers between devices with their start and end apart: 3 -> 5, of which waited for: 3 -> 5; matrix products, arithmetic and copies ran while one was open for 5% -> 0% of each run, Pallas kernels for 0% -> 5%
where the time goes in v1:
time: 112 us
  starting transfers between devices  37 us (33%)
  waiting for transfers between devices  26.9 us (24%)
  blocking collectives  26.6 us (24%)
  Pallas kernels  19.8 us (18%)
    all_to_all x2, blocking collectives, exchange(): lax.all_to_all(flat, 'rep', split_axis=0, concat_axis=0, tiled=True)  26.6 us
    all_to_all x1, starting transfers between devices, body(): lax.all_to_all(send, 'fsdp', split_axis=0, concat_axis=0, tiled=True)  20.8 us
    ppermute x2, waiting for transfers between devices, swap(): return lax.ppermute(value, ('fsdp', 'rep'), pairs)  10.1 us
    pallas_call x1, Pallas kernels, body(): pl.pallas_call(functools.partial(newton_schulz_kernel, math.sqrt(max(R, w...  9.12 us
    all_to_all x1, waiting for transfers between devices, body(): lax.all_to_all(send, 'fsdp', split_axis=0, concat_axis=0, tiled=True)  7.86 us
    all_to_all x1, starting transfers between devices, body(): lax.all_to_all(back, 'fsdp', split_axis=0, concat_axis=0, tiled=True)  6.4 us
    ppermute x2, starting transfers between devices, swap(): return lax.ppermute(value, ('fsdp', 'rep'), pairs)  5 us
    all_to_all x1, starting transfers between devices, exchange(): lax.all_to_all(flat, 'rep', split_axis=0, concat_axis=0, tiled=True)  4.85 us
  transfers between devices with their start and end apart: 5, of which 5 were waited for; matrix products, arithmetic and copies ran while one was open for 0% of the time, Pallas kernels for 5%

profile of v1, /device:TPU:1, one launch (start us, length us, event | category | flops | bytes accessed | tf_op | source)
XLA Modules:
  0.0 111.9 jit_solution(2278105286376386936)
XLA Ops:
  0.6 0.0 copy-start
  0.6 0.0 copy-start.1
  0.7 0.0 copy-start.2
  0.7 2.1 %split.1 = bf16[4,576,128]{2,1,0:T(8,128)(2,1)} custom-call(f32[72,4,1024]{2,1,0:T(4,128)} %bitcast.13), custom_call_target="tpu_custom_call" | custom-call | bytes 2000000 | tf_op jit(solution)/shard_map/split/pallas_call | solution.py:262
  2.8 4.9 %all-to-all-start = ((bf16[4,576,128]{2,1,0:T(8,128)(2,1)}), bf16[4,576,128]{2,1,0:T(8,128)(2,1)S(1)}, u32[]{:S(2)}, u32[]{:S(2)}) async-start(bf16[4,576,128]{2,1,0:T(8,128)(2,1)} %split.1), calls=%async_computation | async-start | bytes 1179648 | tf_op jit(solution)/shard_map/all_to_all | solution.py:249
  7.6 0.0 copy-done
  7.6 0.0 copy-done.1
  7.6 0.0 copy-done.2
  7.6 2.3 %own.1 = (f32[576,128]{1,0:T(8,128)S(1)}, bf16[384,1024]{1,0:T(8,128)(2,1)S(1)}, bf16[1024,384]{1,0:T(8,128)(2,1)S(1)}) custom-call(s32[72]{0:T(128)S(1)} %copy-done.2, s32[72,128]{1,0:T(8,128)S(1)} %copy-done.1, f32[72,4,1024]{2,1,0:T(4,128)S(1)} %bitcast.9), custom_call_target="tpu_custom_call" | custom-call | bytes 4000000 | tf_op jit(solution)/shard_map/own/pallas_call | solution.py:279
  10.0 0.0 copy-start.3
  10.0 0.9 copy-done.3
  10.8 4.1 %all-to-all-done.parts_ref = bf16[4,576,128]{2,1,0:T(8,128)(2,1)S(1)} async-done(((bf16[4,576,128]{2,1,0:T(8,128)(2,1)}), bf16[4,576,128]{2,1,0:T(8,128)(2,1)S(1)}, u32[]{:S(2)}, u32[]{:S(2)}) %all-to-all-start) | async-done | bytes 589856 | tf_op jit(solution)/shard_map/all_to_all | solution.py:249
  14.9 1.5 %scatter.1 = (bf16[1024,128]{1,0:T(8,128)(2,1)}, bf16[576,128]{1,0:T(8,128)(2,1)S(1)}) custom-call(s32[72]{0:T(128)S(1)} %copy-done.2, f32[576,128]{1,0:T(8,128)S(1)} %get-tuple-element.13.base_ref, bf16[4,576,128]{2,1,0:T(8,128)(2,1)S(1)} %all-to-all-done.parts_ref), custom_call_target="tpu_custom_call" | custom-call | bytes 2000000 | tf_op jit(solution)/shard_map/scatter/pallas_call | solution.py:289
  16.4 20.8 %all-to-all-start.1 = ((bf16[128,8,128]{2,1,0:T(8,128)(2,1)}), bf16[128,8,128]{2,1,0:T(8,128)(2,1)S(1)}, u32[]{:S(2)}, u32[]{:S(2)}) async-start(bf16[128,8,128]{2,1,0:T(8,128)(2,1)} %bitcast.2), calls=%async_computation.1 | async-start | bytes 524288 | tf_op jit(solution)/shard_map/all_to_all | solution.py:300
  37.1 2.8 %collective-permute-start = (bf16[576,128]{1,0:T(8,128)(2,1)S(1)}, bf16[576,128]{1,0:T(8,128)(2,1)S(1)}, u32[]{:S(2)}, u32[]{:S(2)}) collective-permute-start(bf16[576,128]{1,0:T(8,128)(2,1)S(1)} %get-tuple-element.14.total_ref.own_ref), channel_id=1, source_target_pairs={{0,1},{1,0},{2,3},{3,2},{4,7},{5,6},{6,5},{7,4},{8,9},{9,8},{10,11... | collective-permute-start | bytes 442376 | tf_op jit(solution)/shard_map/ppermute | solution.py:244
  39.9 4.6 %collective-permute-done._.first_ref = bf16[576,128]{1,0:T(8,128)(2,1)S(1)} collective-permute-done((bf16[576,128]{1,0:T(8,128)(2,1)S(1)}, bf16[576,128]{1,0:T(8,128)(2,1)S(1)}, u32[]{:S(2)}, u32[]{:S(2)}) %collective-permute-start) | collective-permute-done | bytes 147488 | tf_op jit(solution)/shard_map/ppermute | solution.py:244
  44.5 7.9 %all-to-all-done.1 = bf16[128,8,128]{2,1,0:T(8,128)(2,1)S(1)} async-done(((bf16[128,8,128]{2,1,0:T(8,128)(2,1)}), bf16[128,8,128]{2,1,0:T(8,128)(2,1)S(1)}, u32[]{:S(2)}, u32[]{:S(2)}) %all-to-all-start.1) | async-done | bytes 262176 | tf_op jit(solution)/shard_map/all_to_all | solution.py:300
  52.4 0.4 compact.1
  52.8 0.0 copy-start.4
  52.8 14.6 %all_to_all.40.pieces_ref = bf16[4,384,256]{2,1,0:T(8,128)(2,1)S(1)} all-to-all(bf16[4,384,256]{2,1,0:T(8,128)(2,1)S(1)} %compact.1), channel_id=1, replica_groups=mesh['fsdp'=128,'rep'=4] {'rep'}, dimensions={0} | all-to-all | bytes 1572864 | tf_op jit(solution)/shard_map/all_to_all | solution.py:249
  67.4 0.0 copy-done.4
  67.4 9.1 %newton_schulz.1 = (bf16[384,1024]{1,0:T(8,128)(2,1)}, bf16[1024,128]{1,0:T(8,128)(2,1)}, bf16[1152,128]{1,0:T(8,128)(2,1)S(1)}) custom-call(bf16[1024,384]{1,0:T(8,128)(2,1)S(1)} %copy-done.4, bf16[4,384,256]{2,1,0:T(8,128)(2,1)S(1)} %all_to_all.40.pieces_ref, bf16[576,128]{1,0:T(8,128)(2,1)S(1)} %get-tuple-element.14.total_ref.own_ref, ...), custom_call_target="tpu_custom_call" | custom-call | flops 5000000000 | bytes 4000000 | tf_op jit(solution)/shard_map/newton_schulz/pallas_call | solution.py:312
  76.5 6.4 %all-to-all-start.3 = ((bf16[128,8,128]{2,1,0:T(8,128)(2,1)}), bf16[128,8,128]{2,1,0:T(8,128)(2,1)S(1)}, u32[]{:S(2)}, u32[]{:S(2)}) async-start(bf16[128,8,128]{2,1,0:T(8,128)(2,1)} %bitcast.5), calls=%async_computation.3 | async-start | bytes 524288 | tf_op jit(solution)/shard_map/all_to_all | solution.py:322
  82.9 2.2 %collective-permute-start.1 = (bf16[1152,128]{1,0:T(8,128)(2,1)S(1)}, bf16[1152,128]{1,0:T(8,128)(2,1)S(1)}, u32[]{:S(2)}, u32[]{:S(2)}) collective-permute-start(bf16[1152,128]{1,0:T(8,128)(2,1)S(1)} %get-tuple-element.18), channel_id=1, source_target_pairs={{0,3},{1,2},{2,1},{3,0},{4,5},{5,4},{6,7},{7,6},{8,11},{9,10},{10,... | collective-permute-start | bytes 884744 | tf_op jit(solution)/shard_map/ppermute | solution.py:244
  85.2 5.6 %collective-permute-done.1.second_ref = bf16[1152,128]{1,0:T(8,128)(2,1)S(1)} collective-permute-done((bf16[1152,128]{1,0:T(8,128)(2,1)S(1)}, bf16[1152,128]{1,0:T(8,128)(2,1)S(1)}, u32[]{:S(2)}, u32[]{:S(2)}) %collective-permute-start.1) | collective-permute-done | bytes 294944 | tf_op jit(solution)/shard_map/ppermute | solution.py:244
  90.7 2.8 %momentum.1 = (f32[72,4,1024]{2,1,0:T(4,128)}, f32[8,128]{1,0:T(8,128)S(1)}) custom-call(s32[72,128]{1,0:T(8,128)S(1)} %copy-done.1, f32[72,4,1024]{2,1,0:T(4,128)S(1)} %bitcast.10, bf16[576,128]{1,0:T(8,128)(2,1)S(1)} %get-tuple-element.14.total_ref.own_ref, bf16[576,128]{1,0:T(8,128)(2,1)S(1)} %collective-permute-done._.first_ref, ...), custom_call_target="tpu_custom_call" | custom-call | bytes 4000000 | tf_op jit(solution)/shard_map/momentum/pallas_call | solution.py:323
  93.5 4.8 %all-to-all-done.3 = bf16[128,8,128]{2,1,0:T(8,128)(2,1)S(1)} async-done(((bf16[128,8,128]{2,1,0:T(8,128)(2,1)}), bf16[128,8,128]{2,1,0:T(8,128)(2,1)S(1)}, u32[]{:S(2)}, u32[]{:S(2)}) %all-to-all-start.3) | async-done | bytes 262176 | tf_op jit(solution)/shard_map/all_to_all | solution.py:322
  98.3 0.6 select.1
  98.9 12.0 %all_to_all.41.pieces_ref = bf16[4,576,128]{2,1,0:T(8,128)(2,1)S(1)} all-to-all(bf16[4,576,128]{2,1,0:T(8,128)(2,1)S(1)} %select.1), channel_id=1, replica_groups=mesh['fsdp'=128,'rep'=4] {'rep'}, dimensions={0} | all-to-all | bytes 1179648 | tf_op jit(solution)/shard_map/all_to_all | solution.py:249
  110.9 1.0 update.1
Async XLA Ops:
  0.6 7.0 %copy-start = (f32[1,72,4,1024]{3,2,1,0:T(4,128)S(1)}, f32[1,72,4,1024]{3,2,1,0:T(4,128)}, u32[]{:S(2)}) copy-start(f32[1,72,4,1024]{3,2,1,0:T(4,128)} %param.5) | copy-start | bytes 3538948
  0.6 7.0 %copy-start.1 = (s32[72,128]{1,0:T(8,128)S(1)}, s32[72,128]{1,0:T(8,128)}, u32[]{:S(2)}) copy-start(s32[72,128]{1,0:T(8,128)} %lens_ref.3) | copy-start | bytes 110596
  0.7 7.0 %copy-start.2 = (s32[72]{0:T(128)S(1)}, s32[72]{0:T(128)}, u32[]{:S(2)}) copy-start(s32[72]{0:T(128)} %owner_ref.5) | copy-start | bytes 868
  2.8 12.1 %all-to-all-start = ((bf16[4,576,128]{2,1,0:T(8,128)(2,1)}), bf16[4,576,128]{2,1,0:T(8,128)(2,1)S(1)}, u32[]{:S(2)}, u32[]{:S(2)}) async-start(bf16[4,576,128]{2,1,0:T(8,128)(2,1)} %split.1), calls=%async_computation | async-start | bytes 1179648 | tf_op jit(solution)/shard_map/all_to_all | solution.py:249
  10.0 0.9 copy-start.3
  16.4 36.0 %all-to-all-start.1 = ((bf16[128,8,128]{2,1,0:T(8,128)(2,1)}), bf16[128,8,128]{2,1,0:T(8,128)(2,1)S(1)}, u32[]{:S(2)}, u32[]{:S(2)}) async-start(bf16[128,8,128]{2,1,0:T(8,128)(2,1)} %bitcast.2), calls=%async_computation.1 | async-start | bytes 524288 | tf_op jit(solution)/shard_map/all_to_all | solution.py:300
  37.1 7.4 %collective-permute-start = (bf16[576,128]{1,0:T(8,128)(2,1)S(1)}, bf16[576,128]{1,0:T(8,128)(2,1)S(1)}, u32[]{:S(2)}, u32[]{:S(2)}) collective-permute-start(bf16[576,128]{1,0:T(8,128)(2,1)S(1)} %get-tuple-element.14.total_ref.own_ref), channel_id=1, source_target_pairs={{0,1},{1,0},{2,3},{3,2},{4,7},{5,6},{6,5},{7,4},{8,9},{9,8},{10,11... | collective-permute-start | bytes 442376 | tf_op jit(solution)/shard_map/ppermute | solution.py:244
  52.8 14.6 %copy-start.4 = (bf16[1024,384]{1,0:T(8,128)(2,1)S(1)}, bf16[1024,384]{1,0:T(8,128)(2,1)}, u32[]{:S(2)}) copy-start(bf16[1024,384]{1,0:T(8,128)(2,1)} %copy-done.3) | copy-start | bytes 2359300
  76.5 21.7 %all-to-all-start.3 = ((bf16[128,8,128]{2,1,0:T(8,128)(2,1)}), bf16[128,8,128]{2,1,0:T(8,128)(2,1)S(1)}, u32[]{:S(2)}, u32[]{:S(2)}) async-start(bf16[128,8,128]{2,1,0:T(8,128)(2,1)} %bitcast.5), calls=%async_computation.3 | async-start | bytes 524288 | tf_op jit(solution)/shard_map/all_to_all | solution.py:322
  82.9 7.8 %collective-permute-start.1 = (bf16[1152,128]{1,0:T(8,128)(2,1)S(1)}, bf16[1152,128]{1,0:T(8,128)(2,1)S(1)}, u32[]{:S(2)}, u32[]{:S(2)}) collective-permute-start(bf16[1152,128]{1,0:T(8,128)(2,1)S(1)} %get-tuple-element.18), channel_id=1, source_target_pairs={{0,3},{1,2},{2,1},{3,0},{4,5},{5,4},{6,7},{7,6},{8,11},{9,10},{10,... | collective-permute-start | bytes 884744 | tf_op jit(solution)/shard_map/ppermute | solution.py:244

commit v2 on v1

--- a/solution.py
+++ b/solution.py
@@ -150,37 +150,74 @@
         out_ref[rep] = picked
 
 
-def newton_schulz_kernel(scale, place_ref, pieces_ref, total_ref, first_ref, owned_ref, back_ref, joined_ref, matrix, x):
+def newton_schulz_kernel(scale, pieces_ref, scaled_ref, x, gram, poly):
+    wide = 2 * LANES
+    blocks, rows = pieces_ref.shape[:2]
+    tiles = [slice(block * wide, (block + 1) * wide) for block in range(blocks)]
+    fold = rows // 4
+    low = rows * 2 // 3
+    partial = jnp.zeros((fold, wide), F32)
+    for at in range(0, rows, fold):
+        squares = [pieces_ref[block, at:at + fold, :].astype(F32) for block in range(blocks)]
+        squares = [piece * piece for piece in squares]
+        partial = partial + ((squares[0] + squares[1]) + (squares[2] + squares[3]))
+    factor = 1.0 / (jnp.sqrt(jnp.full((1, wide), jnp.sum(partial), F32)) + 1e-07)
+    for block, tile in enumerate(tiles):
+        x[:, tile] = (pieces_ref[block].astype(F32) * factor).astype(BF16)
+
+    def poly_of():
+        contract = (((1,), (1,)), ((), ()))
+        for at, left in ((0, x[...]), (low, x[low:, :])):
+            right = x[at:at + low, :]
+            part = lax.dot_general(left, right, contract, preferred_element_type=F32)
+            gram[at:, at:at + low] = part.astype(BF16)
+            if at == 0:
+                gram[:low, low:] = part[low:, :].T.astype(BF16)
+        for at in (0, low):
+            part = jnp.dot(gram[at:, :], gram[:, at:at + low], preferred_element_type=F32)
+            part = COEF_B * gram[at:, at:at + low].astype(F32) + COEF_C * part
+            poly[at:, at:at + low] = part.astype(BF16)
+            if at == 0:
+                poly[:low, low:] = part[low:, :].T.astype(BF16)
+        return poly[...]
+
+    def next_of(now, tile):
+        part = x[:, tile]
+        return (COEF_A * part.astype(F32) + jnp.dot(now, part, preferred_element_type=F32)).astype(BF16)
+
+    def step(index, carry):
+        now = poly_of()
+        for tile in tiles:
+            x[:, tile] = next_of(now, tile)
+        return carry
+
+    lax.fori_loop(0, ITERS - 1, step, 0)
+    last = poly_of()
+    for tile in tiles:
+        scaled_ref[:, tile] = (-scale * next_of(last, tile).astype(F32)).astype(BF16)
+
+
+def place_kernel(place_ref, scaled_ref, total_ref, first_ref, back_ref, joined_ref, back, sems):
     rows8 = total_ref.shape[0]
+    mine = scaled_ref[:, pl.ds(column_of(0, lax.axis_index("rep")), 2 * LANES)]
+    some = back_ref.shape[0] // 2
+    upper = in_half((some, LANES), 0)
+    copies = []
+    for half in range(2):
+        at = slice(half * some, (half + 1) * some)
+        spread = jnp.dot(place_ref[at, :], mine, preferred_element_type=F32)
+        back[at, :] = jnp.where(upper, spread[:, :LANES], spread[:, LANES:]).astype(BF16)
+        copies.append(pltpu.make_async_copy(back.at[at], back_ref.at[at], sems.at[half]))
+        copies[-1].start()
     joined_ref[:rows8, :] = total_ref[...]
     joined_ref[rows8:, :] = first_ref[...]
-    me = lax.axis_index("rep")
-    wide = 2 * LANES
-    upper = in_half((place_ref.shape[0], LANES), 0)
-    for block in range(pieces_ref.shape[0]):
-        matrix[:, block * wide:(block + 1) * wide] = pieces_ref[block].astype(F32)
-    squares = jnp.sum(matrix[...] * matrix[...])
-    factor = 1.0 / (jnp.sqrt(jnp.full((1, LANES), squares, F32)) + 1e-07)
-    for tile in range(matrix.shape[1] // LANES):
-        at = slice(tile * LANES, (tile + 1) * LANES)
-        x[:, at] = (matrix[:, at] * factor).astype(BF16)
-
-    def step(index, carry):
-        contract = (((1,), (1,)), ((), ()))
-        gram = lax.dot_general(x[...], x[...], contract, preferred_element_type=F32).astype(BF16)
-        square = jnp.dot(gram, gram, preferred_element_type=F32)
-        poly = (COEF_B * gram.astype(F32) + COEF_C * square).astype(BF16)
-        for tile in range(x.shape[1] // wide):
-            at = slice(tile * wide, (tile + 1) * wide)
-            part = x[:, at]
-            x[:, at] = (COEF_A * part.astype(F32) + jnp.dot(poly, part, preferred_element_type=F32)).astype(BF16)
-        return carry
-
-    lax.fori_loop(0, ITERS, step, 0)
-    owned_ref[...] = (-scale * x[...].astype(F32)).astype(BF16)
-    mine = owned_ref[:, pl.ds(column_of(0, me), wide)]
-    spread = jnp.dot(place_ref[...], mine, preferred_element_type=F32)
-    back_ref[...] = jnp.where(upper, spread[:, :LANES], spread[:, LANES:]).astype(BF16)
+    for copy in copies:
+        copy.wait()
+
+
+def owned_kernel(scaled_ref, _, owned_ref, done_ref):
+    owned_ref[...] = scaled_ref[...]
+    done_ref[...] = jnp.zeros_like(done_ref)
 
 
 def select_kernel(owner_ref, back_ref, _, out_ref, wide, chosen):
@@ -223,7 +260,7 @@
         out_ref[:, :, at] = got.astype(BF16)
 
 
-def momentum_kernel(lens_ref, mom_ref, own_ref, first_ref, second_ref, out_ref, done_ref, total):
+def momentum_kernel(lens_ref, mom_ref, own_ref, first_ref, second_ref, _, out_ref, done_ref, total):
     done_ref[...] = jnp.zeros_like(done_ref)
     device = lax.axis_index("fsdp")
     count, slots, width = out_ref.shape
@@ -309,27 +346,46 @@
     )(pick, incoming, first)
 
     pieces = exchange(compact)
-    owned, back, joined = pl.pallas_call(
+    scaled = pl.pallas_call(
         functools.partial(newton_schulz_kernel, math.sqrt(max(R, width))),
-        out_shape=[shape((R, width), BF16), shape((slots8, LANES), BF16), shape((2 * rows8, LANES), BF16)],
-        in_specs=[vmem()] * 4,
-        out_specs=[vmem()] * 3,
-        scratch_shapes=[pltpu.VMEM((R, width), F32), pltpu.VMEM((R, width), BF16)],
+        out_shape=shape((R, width), BF16),
+        in_specs=[vmem()],
+        out_specs=vmem(),
+        scratch_shapes=[pltpu.VMEM((R, width), BF16), pltpu.VMEM((R, R), BF16), pltpu.VMEM((R, R), BF16)],
         compiler_params=params(),
         cost_estimate=cost(5_000_000_000, 4_000_000),
         name="newton_schulz",
-    )(place, pieces, total, first)
+    )(pieces)
+    back, joined = pl.pallas_call(
+        place_kernel,
+        out_shape=[shape((slots8, LANES), BF16), shape((2 * rows8, LANES), BF16)],
+        in_specs=[vmem()] * 4,
+        out_specs=[hbm(), vmem()],
+        scratch_shapes=[pltpu.VMEM((slots8, LANES), BF16), pltpu.SemaphoreType.DMA((2,))],
+        compiler_params=params(),
+        cost_estimate=cost(200_000_000, 2_000_000),
+        name="place",
+    )(place, scaled, total, first)
+    owned, written = pl.pallas_call(
+        owned_kernel,
+        out_shape=[shape((R, width), BF16), shape((8, LANES), F32)],
+        in_specs=[vmem(), later()],
+        out_specs=[vmem()] * 2,
+        compiler_params=params(),
+        cost_estimate=cost(0, 2_000_000),
+        name="owned",
+    )(scaled, joined)
     returned = lax.all_to_all(back, "fsdp", split_axis=0, concat_axis=0, tiled=True)
     new_momentum, done = pl.pallas_call(
         momentum_kernel,
         out_shape=[shape((count, slots, width), F32), shape((8, LANES), F32)],
-        in_specs=[smem()] + [vmem()] * 4,
+        in_specs=[smem()] + [vmem()] * 4 + [later()],
         out_specs=[vmem()] * 2,
         scratch_shapes=[pltpu.VMEM((count, slots, width), F32)],
         compiler_params=params(),
         cost_estimate=cost(0, 4_000_000),
         name="momentum",
-    )(lengths, mom, total, first, swap(joined, 1))
+    )(lengths, mom, total, first, swap(joined, 1), written)
     chosen = pl.pallas_call(
         select_kernel,
         out_shape=parts,

time: 112 us -> 114 us (1.018)
  local copies, waits for them, and re-layouts: 0.89 us -> 2.72 us
    pallas_call x0 -> x2, Pallas kernels: none -> 2.15 us  [the longest x1 1.22 us: body(): pl.pallas_call(place_kernel, out_shape=[shape((slots8, LANES), BF16), sha...]
    unnamed x10 -> x12, local copies, waits for them, and re-layouts: 0.89 us -> 2.72 us
    pallas_call x1, Pallas kernels: 9.12 us -> 7.62 us  [body(): pl.pallas_call(functools.partial(newton_schulz_kernel, math.sqrt(max(R, w...]
where the time goes in v2:
time: 114 us; the launch traced here: 113 us
  starting transfers between devices  37 us (32%)
  blocking collectives  26.5 us (23%)
  waiting for transfers between devices  25.9 us (23%)
  Pallas kernels  20.4 us (18%)
  local copies, waits for them, and re-layouts  2.72 us (2%)
    all_to_all x2, blocking collectives, exchange(): lax.all_to_all(flat, 'rep', split_axis=0, concat_axis=0, tiled=True)  26.5 us
    all_to_all x1, starting transfers between devices, body(): lax.all_to_all(send, 'fsdp', split_axis=0, concat_axis=0, tiled=True)  20.8 us
    ppermute x2, waiting for transfers between devices, swap(): return lax.ppermute(value, ('fsdp', 'rep'), pairs)  9.21 us
    all_to_all x1, waiting for transfers between devices, body(): lax.all_to_all(send, 'fsdp', split_axis=0, concat_axis=0, tiled=True)  7.86 us
    pallas_call x1, Pallas kernels, body(): pl.pallas_call(functools.partial(newton_schulz_kernel, math.sqrt(max(R, w...  7.62 us
    all_to_all x1, starting transfers between devices, body(): lax.all_to_all(back, 'fsdp', split_axis=0, concat_axis=0, tiled=True)  6.41 us
    ppermute x2, starting transfers between devices, swap(): return lax.ppermute(value, ('fsdp', 'rep'), pairs)  5 us
    all_to_all x1, starting transfers between devices, exchange(): lax.all_to_all(flat, 'rep', split_axis=0, concat_axis=0, tiled=True)  4.85 us
  transfers between devices with their start and end apart: 5, of which 5 were waited for; matrix products, arithmetic and copies ran while one was open for 0% of the time, Pallas kernels for 5%

profile of v2, /device:TPU:1, one launch (start us, length us, event | category | flops | bytes accessed | tf_op | source)
XLA Modules:
  0.0 113.3 jit_solution(16231554489495250904)
XLA Ops:
  0.6 0.0 copy-start
  0.6 0.0 copy-start.4
  0.7 0.0 copy-start.5
  0.7 2.1 %split.1 = bf16[4,576,128]{2,1,0:T(8,128)(2,1)} custom-call(f32[72,4,1024]{2,1,0:T(4,128)} %bitcast.14), custom_call_target="tpu_custom_call" | custom-call | bytes 2000000 | tf_op jit(solution)/shard_map/split/pallas_call | solution.py:299
  2.8 4.9 %all-to-all-start = ((bf16[4,576,128]{2,1,0:T(8,128)(2,1)}), bf16[4,576,128]{2,1,0:T(8,128)(2,1)S(1)}, u32[]{:S(2)}, u32[]{:S(2)}) async-start(bf16[4,576,128]{2,1,0:T(8,128)(2,1)} %split.1), calls=%async_computation | async-start | bytes 1179648 | tf_op jit(solution)/shard_map/all_to_all | solution.py:286
  7.6 0.0 copy-done
  7.6 0.0 copy-done.4
  7.6 0.0 copy-done.5
  7.6 2.3 %own.1 = (f32[576,128]{1,0:T(8,128)S(1)}, bf16[384,1024]{1,0:T(8,128)(2,1)S(1)}, bf16[1024,384]{1,0:T(8,128)(2,1)S(1)}) custom-call(s32[72]{0:T(128)S(1)} %copy-done.5, s32[72,128]{1,0:T(8,128)S(1)} %copy-done.4, f32[72,4,1024]{2,1,0:T(4,128)S(1)} %bitcast.9), custom_call_target="tpu_custom_call" | custom-call | bytes 4000000 | tf_op jit(solution)/shard_map/own/pallas_call | solution.py:316
  10.0 0.0 copy-start.1
  10.0 0.9 copy-done.1
  10.8 4.1 %all-to-all-done.parts_ref = bf16[4,576,128]{2,1,0:T(8,128)(2,1)S(1)} async-done(((bf16[4,576,128]{2,1,0:T(8,128)(2,1)}), bf16[4,576,128]{2,1,0:T(8,128)(2,1)S(1)}, u32[]{:S(2)}, u32[]{:S(2)}) %all-to-all-start) | async-done | bytes 589856 | tf_op jit(solution)/shard_map/all_to_all | solution.py:286
  14.9 1.5 %scatter.1 = (bf16[1024,128]{1,0:T(8,128)(2,1)}, bf16[576,128]{1,0:T(8,128)(2,1)S(1)}) custom-call(s32[72]{0:T(128)S(1)} %copy-done.5, f32[576,128]{1,0:T(8,128)S(1)} %get-tuple-element.14.base_ref, bf16[4,576,128]{2,1,0:T(8,128)(2,1)S(1)} %all-to-all-done.parts_ref), custom_call_target="tpu_custom_call" | custom-call | bytes 2000000 | tf_op jit(solution)/shard_map/scatter/pallas_call | solution.py:326
  16.4 20.8 %all-to-all-start.1 = ((bf16[128,8,128]{2,1,0:T(8,128)(2,1)}), bf16[128,8,128]{2,1,0:T(8,128)(2,1)S(1)}, u32[]{:S(2)}, u32[]{:S(2)}) async-start(bf16[128,8,128]{2,1,0:T(8,128)(2,1)} %bitcast.2), calls=%async_computation.1 | async-start | bytes 524288 | tf_op jit(solution)/shard_map/all_to_all | solution.py:337
  37.1 2.8 %collective-permute-start = (bf16[576,128]{1,0:T(8,128)(2,1)S(1)}, bf16[576,128]{1,0:T(8,128)(2,1)S(1)}, u32[]{:S(2)}, u32[]{:S(2)}) collective-permute-start(bf16[576,128]{1,0:T(8,128)(2,1)S(1)} %get-tuple-element.15.total_ref.own_ref), channel_id=1, source_target_pairs={{0,1},{1,0},{2,3},{3,2},{4,7},{5,6},{6,5},{7,4},{8,9},{9,8},{10,11... | collective-permute-start | bytes 442376 | tf_op jit(solution)/shard_map/ppermute | solution.py:281
  39.9 4.6 %collective-permute-done._.first_ref = bf16[576,128]{1,0:T(8,128)(2,1)S(1)} collective-permute-done((bf16[576,128]{1,0:T(8,128)(2,1)S(1)}, bf16[576,128]{1,0:T(8,128)(2,1)S(1)}, u32[]{:S(2)}, u32[]{:S(2)}) %collective-permute-start) | collective-permute-done | bytes 147488 | tf_op jit(solution)/shard_map/ppermute | solution.py:281
  44.5 7.9 %all-to-all-done.1 = bf16[128,8,128]{2,1,0:T(8,128)(2,1)S(1)} async-done(((bf16[128,8,128]{2,1,0:T(8,128)(2,1)}), bf16[128,8,128]{2,1,0:T(8,128)(2,1)S(1)}, u32[]{:S(2)}, u32[]{:S(2)}) %all-to-all-start.1) | async-done | bytes 262176 | tf_op jit(solution)/shard_map/all_to_all | solution.py:337
  52.4 0.0 copy-start.2
  52.4 1.1 copy-done.2
  53.5 0.4 compact.1
  54.0 14.4 %all_to_all.40.pieces_ref = bf16[4,384,256]{2,1,0:T(8,128)(2,1)S(1)} all-to-all(bf16[4,384,256]{2,1,0:T(8,128)(2,1)S(1)} %compact.1), channel_id=1, replica_groups=mesh['fsdp'=128,'rep'=4] {'rep'}, dimensions={0} | all-to-all | bytes 1572864 | tf_op jit(solution)/shard_map/all_to_all | solution.py:286
  68.4 7.6 %newton_schulz.1.scaled_ref = bf16[384,1024]{1,0:T(8,128)(2,1)S(1)} custom-call(bf16[4,384,256]{2,1,0:T(8,128)(2,1)S(1)} %all_to_all.40.pieces_ref), custom_call_target="tpu_custom_call" | custom-call | flops 5000000000 | bytes 4000000 | tf_op jit(solution)/shard_map/newton_schulz/pallas_call | solution.py:349
  76.0 1.2 %place.1 = (bf16[1024,128]{1,0:T(8,128)(2,1)S(1)}, bf16[1152,128]{1,0:T(8,128)(2,1)S(1)}) custom-call(bf16[1024,384]{1,0:T(8,128)(2,1)S(1)} %get-tuple-element.16.place_ref, bf16[384,1024]{1,0:T(8,128)(2,1)S(1)} %newton_schulz.1.scaled_ref, bf16[576,128]{1,0:T(8,128)(2,1)S(1)} %get-tuple-element.15.total_ref.own_ref, ...), custom_call_target="tpu_custom_call" | custom-call | flops 200000000 | bytes 2000000 | tf_op jit(solution)/shard_map/place/pallas_call | solution.py:359
  77.3 0.0 copy-start.3
  77.3 0.7 copy-done.3
  78.0 6.4 %all-to-all-start.3 = ((bf16[128,8,128]{2,1,0:T(8,128)(2,1)}), bf16[128,8,128]{2,1,0:T(8,128)(2,1)S(1)}, u32[]{:S(2)}, u32[]{:S(2)}) async-start(bf16[128,8,128]{2,1,0:T(8,128)(2,1)} %bitcast.13), calls=%async_computation.3 | async-start | bytes 524288 | tf_op jit(solution)/shard_map/all_to_all | solution.py:378
  84.4 2.2 %collective-permute-start.1 = (bf16[1152,128]{1,0:T(8,128)(2,1)S(1)}, bf16[1152,128]{1,0:T(8,128)(2,1)S(1)}, u32[]{:S(2)}, u32[]{:S(2)}) collective-permute-start(bf16[1152,128]{1,0:T(8,128)(2,1)S(1)} %get-tuple-element.19._), channel_id=1, source_target_pairs={{0,3},{1,2},{2,1},{3,0},{4,5},{5,4},{6,7},{7,6},{8,11},{9,10},{10,... | collective-permute-start | bytes 884744 | tf_op jit(solution)/shard_map/ppermute | solution.py:281
  86.6 0.9 owned.1
  87.5 4.6 %collective-permute-done.1.second_ref = bf16[1152,128]{1,0:T(8,128)(2,1)S(1)} collective-permute-done((bf16[1152,128]{1,0:T(8,128)(2,1)S(1)}, bf16[1152,128]{1,0:T(8,128)(2,1)S(1)}, u32[]{:S(2)}, u32[]{:S(2)}) %collective-permute-start.1) | collective-permute-done | bytes 294944 | tf_op jit(solution)/shard_map/ppermute | solution.py:281
  92.1 2.8 %momentum.1 = (f32[72,4,1024]{2,1,0:T(4,128)}, f32[8,128]{1,0:T(8,128)S(1)}) custom-call(s32[72,128]{1,0:T(8,128)S(1)} %copy-done.4, f32[72,4,1024]{2,1,0:T(4,128)S(1)} %bitcast.10, bf16[576,128]{1,0:T(8,128)(2,1)S(1)} %get-tuple-element.15.total_ref.own_ref, bf16[576,128]{1,0:T(8,128)(2,1)S(1)} %collective-permute-done._.first_ref, ...), custom_call_target="tpu_custom_call" | custom-call | bytes 4000000 | tf_op jit(solution)/shard_map/momentum/pallas_call | solution.py:379
  94.9 4.8 %all-to-all-done.3 = bf16[128,8,128]{2,1,0:T(8,128)(2,1)S(1)} async-done(((bf16[128,8,128]{2,1,0:T(8,128)(2,1)}), bf16[128,8,128]{2,1,0:T(8,128)(2,1)S(1)}, u32[]{:S(2)}, u32[]{:S(2)}) %all-to-all-start.3) | async-done | bytes 262176 | tf_op jit(solution)/shard_map/all_to_all | solution.py:378
  99.7 0.6 select.1
  100.3 12.0 %all_to_all.41.pieces_ref = bf16[4,576,128]{2,1,0:T(8,128)(2,1)S(1)} all-to-all(bf16[4,576,128]{2,1,0:T(8,128)(2,1)S(1)} %select.1), channel_id=1, replica_groups=mesh['fsdp'=128,'rep'=4] {'rep'}, dimensions={0} | all-to-all | bytes 1179648 | tf_op jit(solution)/shard_map/all_to_all | solution.py:286
  112.4 1.0 update.1
Async XLA Ops:
  0.6 7.0 %copy-start = (f32[1,72,4,1024]{3,2,1,0:T(4,128)S(1)}, f32[1,72,4,1024]{3,2,1,0:T(4,128)}, u32[]{:S(2)}) copy-start(f32[1,72,4,1024]{3,2,1,0:T(4,128)} %param.5) | copy-start | bytes 3538948
  0.6 7.0 %copy-start.4 = (s32[72,128]{1,0:T(8,128)S(1)}, s32[72,128]{1,0:T(8,128)}, u32[]{:S(2)}) copy-start(s32[72,128]{1,0:T(8,128)} %lens_ref.3) | copy-start | bytes 110596
  0.7 7.0 %copy-start.5 = (s32[72]{0:T(128)S(1)}, s32[72]{0:T(128)}, u32[]{:S(2)}) copy-start(s32[72]{0:T(128)} %owner_ref.5) | copy-start | bytes 868
  2.8 12.1 %all-to-all-start = ((bf16[4,576,128]{2,1,0:T(8,128)(2,1)}), bf16[4,576,128]{2,1,0:T(8,128)(2,1)S(1)}, u32[]{:S(2)}, u32[]{:S(2)}) async-start(bf16[4,576,128]{2,1,0:T(8,128)(2,1)} %split.1), calls=%async_computation | async-start | bytes 1179648 | tf_op jit(solution)/shard_map/all_to_all | solution.py:286
  10.0 0.9 copy-start.1
  16.4 36.0 %all-to-all-start.1 = ((bf16[128,8,128]{2,1,0:T(8,128)(2,1)}), bf16[128,8,128]{2,1,0:T(8,128)(2,1)S(1)}, u32[]{:S(2)}, u32[]{:S(2)}) async-start(bf16[128,8,128]{2,1,0:T(8,128)(2,1)} %bitcast.2), calls=%async_computation.1 | async-start | bytes 524288 | tf_op jit(solution)/shard_map/all_to_all | solution.py:337
  37.1 7.4 %collective-permute-start = (bf16[576,128]{1,0:T(8,128)(2,1)S(1)}, bf16[576,128]{1,0:T(8,128)(2,1)S(1)}, u32[]{:S(2)}, u32[]{:S(2)}) collective-permute-start(bf16[576,128]{1,0:T(8,128)(2,1)S(1)} %get-tuple-element.15.total_ref.own_ref), channel_id=1, source_target_pairs={{0,1},{1,0},{2,3},{3,2},{4,7},{5,6},{6,5},{7,4},{8,9},{9,8},{10,11... | collective-permute-start | bytes 442376 | tf_op jit(solution)/shard_map/ppermute | solution.py:281
  52.4 1.1 %copy-start.2 = (bf16[384,1024]{1,0:T(8,128)(2,1)S(1)}, bf16[384,1024]{1,0:T(8,128)(2,1)}, u32[]{:S(2)}) copy-start(bf16[384,1024]{1,0:T(8,128)(2,1)} %copy-done.1) | copy-start | bytes 2359300
  77.3 0.7 copy-start.3
  78.0 21.7 %all-to-all-start.3 = ((bf16[128,8,128]{2,1,0:T(8,128)(2,1)}), bf16[128,8,128]{2,1,0:T(8,128)(2,1)S(1)}, u32[]{:S(2)}, u32[]{:S(2)}) async-start(bf16[128,8,128]{2,1,0:T(8,128)(2,1)} %bitcast.13), calls=%async_computation.3 | async-start | bytes 524288 | tf_op jit(solution)/shard_map/all_to_all | solution.py:378
  84.4 7.8 %collective-permute-start.1 = (bf16[1152,128]{1,0:T(8,128)(2,1)S(1)}, bf16[1152,128]{1,0:T(8,128)(2,1)S(1)}, u32[]{:S(2)}, u32[]{:S(2)}) collective-permute-start(bf16[1152,128]{1,0:T(8,128)(2,1)S(1)} %get-tuple-element.19._), channel_id=1, source_target_pairs={{0,3},{1,2},{2,1},{3,0},{4,5},{5,4},{6,7},{7,6},{8,11},{9,10},{10,... | collective-permute-start | bytes 884744 | tf_op jit(solution)/shard_map/ppermute | solution.py:281

commit v3 on v1

--- a/solution.py
+++ b/solution.py
@@ -19,7 +19,8 @@
 ROWS = 8
 BF16 = jnp.bfloat16
 F32 = jnp.float32
-VMEM_LIMIT = 48 * 1024 * 1024
+VMEM_LIMIT = 24 * 1024 * 1024
+SPLIT_LIMIT = 60 * 1024 * 1024
 
 
 def vmem():
@@ -150,37 +151,52 @@
         out_ref[rep] = picked
 
 
-def newton_schulz_kernel(scale, place_ref, pieces_ref, total_ref, first_ref, owned_ref, back_ref, joined_ref, matrix, x):
+def newton_schulz_kernel(scale, place_ref, pieces_ref, total_ref, first_ref, scaled_ref, back_ref, joined_ref, x):
     rows8 = total_ref.shape[0]
     joined_ref[:rows8, :] = total_ref[...]
     joined_ref[rows8:, :] = first_ref[...]
-    me = lax.axis_index("rep")
     wide = 2 * LANES
-    upper = in_half((place_ref.shape[0], LANES), 0)
-    for block in range(pieces_ref.shape[0]):
-        matrix[:, block * wide:(block + 1) * wide] = pieces_ref[block].astype(F32)
-    squares = jnp.sum(matrix[...] * matrix[...])
-    factor = 1.0 / (jnp.sqrt(jnp.full((1, LANES), squares, F32)) + 1e-07)
-    for tile in range(matrix.shape[1] // LANES):
-        at = slice(tile * LANES, (tile + 1) * LANES)
-        x[:, at] = (matrix[:, at] * factor).astype(BF16)
-
-    def step(index, carry):
+    blocks, rows = pieces_ref.shape[:2]
+    tiles = [slice(block * wide, (block + 1) * wide) for block in range(blocks)]
+    fold = rows // 4
+    partial = jnp.zeros((fold, wide), F32)
+    for at in range(0, rows, fold):
+        squares = [pieces_ref[block, at:at + fold, :].astype(F32) for block in range(blocks)]
+        squares = [piece * piece for piece in squares]
+        partial = partial + ((squares[0] + squares[1]) + (squares[2] + squares[3]))
+    factor = 1.0 / (jnp.sqrt(jnp.full((1, wide), jnp.sum(partial), F32)) + 1e-07)
+    for block, tile in enumerate(tiles):
+        x[:, tile] = (pieces_ref[block].astype(F32) * factor).astype(BF16)
+
+    def poly_of():
         contract = (((1,), (1,)), ((), ()))
         gram = lax.dot_general(x[...], x[...], contract, preferred_element_type=F32).astype(BF16)
         square = jnp.dot(gram, gram, preferred_element_type=F32)
-        poly = (COEF_B * gram.astype(F32) + COEF_C * square).astype(BF16)
-        for tile in range(x.shape[1] // wide):
-            at = slice(tile * wide, (tile + 1) * wide)
-            part = x[:, at]
-            x[:, at] = (COEF_A * part.astype(F32) + jnp.dot(poly, part, preferred_element_type=F32)).astype(BF16)
+        return (COEF_B * gram.astype(F32) + COEF_C * square).astype(BF16)
+
+    def next_of(poly, tile):
+        part = x[:, tile]
+        return (COEF_A * part.astype(F32) + jnp.dot(poly, part, preferred_element_type=F32)).astype(BF16)
+
+    def step(index, carry):
+        poly = poly_of()
+        for tile in tiles:
+            x[:, tile] = next_of(poly, tile)
         return carry
 
-    lax.fori_loop(0, ITERS, step, 0)
-    owned_ref[...] = (-scale * x[...].astype(F32)).astype(BF16)
-    mine = owned_ref[:, pl.ds(column_of(0, me), wide)]
+    lax.fori_loop(0, ITERS - 1, step, 0)
+    poly = poly_of()
+    for tile in tiles:
+        scaled_ref[:, tile] = (-scale * next_of(poly, tile).astype(F32)).astype(BF16)
+    mine = scaled_ref[:, pl.ds(column_of(0, lax.axis_index("rep")), wide)]
+    upper = in_half((place_ref.shape[0], LANES), 0)
     spread = jnp.dot(place_ref[...], mine, preferred_element_type=F32)
     back_ref[...] = jnp.where(upper, spread[:, :LANES], spread[:, LANES:]).astype(BF16)
+
+
+def owned_kernel(scaled_ref, _, owned_ref, done_ref):
+    owned_ref[...] = scaled_ref[...]
+    done_ref[...] = jnp.zeros_like(done_ref)
 
 
 def select_kernel(owner_ref, back_ref, _, out_ref, wide, chosen):
@@ -223,7 +239,7 @@
         out_ref[:, :, at] = got.astype(BF16)
 
 
-def momentum_kernel(lens_ref, mom_ref, own_ref, first_ref, second_ref, out_ref, done_ref, total):
+def momentum_kernel(lens_ref, mom_ref, own_ref, first_ref, second_ref, _, out_ref, done_ref, total):
     done_ref[...] = jnp.zeros_like(done_ref)
     device = lax.axis_index("fsdp")
     count, slots, width = out_ref.shape
@@ -271,7 +287,7 @@
             pltpu.SemaphoreType.DMA((reps,)),
             pltpu.SemaphoreType.DMA((reps,)),
         ],
-        compiler_params=params(60 * 1024 * 1024),
+        compiler_params=params(SPLIT_LIMIT),
         cost_estimate=cost(0, 2_000_000),
         name="split",
     )(g)
@@ -309,27 +325,36 @@
     )(pick, incoming, first)
 
     pieces = exchange(compact)
-    owned, back, joined = pl.pallas_call(
+    scaled, back, joined = pl.pallas_call(
         functools.partial(newton_schulz_kernel, math.sqrt(max(R, width))),
         out_shape=[shape((R, width), BF16), shape((slots8, LANES), BF16), shape((2 * rows8, LANES), BF16)],
         in_specs=[vmem()] * 4,
         out_specs=[vmem()] * 3,
-        scratch_shapes=[pltpu.VMEM((R, width), F32), pltpu.VMEM((R, width), BF16)],
+        scratch_shapes=[pltpu.VMEM((R, width), BF16)],
         compiler_params=params(),
         cost_estimate=cost(5_000_000_000, 4_000_000),
         name="newton_schulz",
     )(place, pieces, total, first)
+    owned, written = pl.pallas_call(
+        owned_kernel,
+        out_shape=[shape((R, width), BF16), shape((8, LANES), F32)],
+        in_specs=[vmem(), later()],
+        out_specs=[vmem()] * 2,
+        compiler_params=params(),
+        cost_estimate=cost(0, 2_000_000),
+        name="owned",
+    )(scaled, joined)
     returned = lax.all_to_all(back, "fsdp", split_axis=0, concat_axis=0, tiled=True)
     new_momentum, done = pl.pallas_call(
         momentum_kernel,
         out_shape=[shape((count, slots, width), F32), shape((8, LANES), F32)],
-        in_specs=[smem()] + [vmem()] * 4,
+        in_specs=[smem()] + [vmem()] * 4 + [later()],
         out_specs=[vmem()] * 2,
         scratch_shapes=[pltpu.VMEM((count, slots, width), F32)],
         compiler_params=params(),
         cost_estimate=cost(0, 4_000_000),
         name="momentum",
-    )(lengths, mom, total, first, swap(joined, 1))
+    )(lengths, mom, total, first, swap(joined, 1), written)
     chosen = pl.pallas_call(
         select_kernel,
         out_shape=parts,

time: 112 us -> 112 us (level)
  no operation moved by 1% of the time
where the time goes in v3:
time: 112 us; the launch traced here: 111 us
  starting transfers between devices  37 us (33%)
  blocking collectives  26.6 us (24%)
  waiting for transfers between devices  26 us (23%)
  Pallas kernels  20.1 us (18%)
    all_to_all x2, blocking collectives, exchange(): lax.all_to_all(flat, 'rep', split_axis=0, concat_axis=0, tiled=True)  26.6 us
    all_to_all x1, starting transfers between devices, body(): lax.all_to_all(send, 'fsdp', split_axis=0, concat_axis=0, tiled=True)  20.8 us
    ppermute x2, waiting for transfers between devices, swap(): return lax.ppermute(value, ('fsdp', 'rep'), pairs)  9.22 us
    pallas_call x1, Pallas kernels, body(): pl.pallas_call(functools.partial(newton_schulz_kernel, math.sqrt(max(R, w...  8.55 us
    all_to_all x1, waiting for transfers between devices, body(): lax.all_to_all(send, 'fsdp', split_axis=0, concat_axis=0, tiled=True)  7.86 us
    all_to_all x1, starting transfers between devices, body(): lax.all_to_all(back, 'fsdp', split_axis=0, concat_axis=0, tiled=True)  6.41 us
    ppermute x2, starting transfers between devices, swap(): return lax.ppermute(value, ('fsdp', 'rep'), pairs)  4.99 us
    all_to_all x1, starting transfers between devices, exchange(): lax.all_to_all(flat, 'rep', split_axis=0, concat_axis=0, tiled=True)  4.85 us
  transfers between devices with their start and end apart: 5, of which 5 were waited for; matrix products, arithmetic and copies ran while one was open for 0% of the time, Pallas kernels for 5%

profile of v3, /device:TPU:1, one launch (start us, length us, event | category | flops | bytes accessed | tf_op | source)
XLA Modules:
  0.0 111.4 jit_solution(8770389611469044781)
XLA Ops:
  0.6 0.0 copy-start
  0.6 0.0 copy-start.1
  0.7 0.0 copy-start.2
  0.7 2.1 %split.1 = bf16[4,576,128]{2,1,0:T(8,128)(2,1)} custom-call(f32[72,4,1024]{2,1,0:T(4,128)} %bitcast.13), custom_call_target="tpu_custom_call" | custom-call | bytes 2000000 | tf_op jit(solution)/shard_map/split/pallas_call | solution.py:278
  2.8 4.9 %all-to-all-start = ((bf16[4,576,128]{2,1,0:T(8,128)(2,1)}), bf16[4,576,128]{2,1,0:T(8,128)(2,1)S(1)}, u32[]{:S(2)}, u32[]{:S(2)}) async-start(bf16[4,576,128]{2,1,0:T(8,128)(2,1)} %split.1), calls=%async_computation | async-start | bytes 1179648 | tf_op jit(solution)/shard_map/all_to_all | solution.py:265
  7.6 0.0 copy-done
  7.6 0.0 copy-done.1
  7.6 0.0 copy-done.2
  7.6 2.3 %own.1 = (f32[576,128]{1,0:T(8,128)S(1)}, bf16[384,1024]{1,0:T(8,128)(2,1)S(1)}, bf16[1024,384]{1,0:T(8,128)(2,1)S(1)}) custom-call(s32[72]{0:T(128)S(1)} %copy-done.2, s32[72,128]{1,0:T(8,128)S(1)} %copy-done.1, f32[72,4,1024]{2,1,0:T(4,128)S(1)} %bitcast.9), custom_call_target="tpu_custom_call" | custom-call | bytes 4000000 | tf_op jit(solution)/shard_map/own/pallas_call | solution.py:295
  10.0 0.0 copy-start.3
  10.0 0.9 copy-done.3
  10.8 4.1 %all-to-all-done.parts_ref = bf16[4,576,128]{2,1,0:T(8,128)(2,1)S(1)} async-done(((bf16[4,576,128]{2,1,0:T(8,128)(2,1)}), bf16[4,576,128]{2,1,0:T(8,128)(2,1)S(1)}, u32[]{:S(2)}, u32[]{:S(2)}) %all-to-all-start) | async-done | bytes 589856 | tf_op jit(solution)/shard_map/all_to_all | solution.py:265
  14.9 1.5 %scatter.1 = (bf16[1024,128]{1,0:T(8,128)(2,1)}, bf16[576,128]{1,0:T(8,128)(2,1)S(1)}) custom-call(s32[72]{0:T(128)S(1)} %copy-done.2, f32[576,128]{1,0:T(8,128)S(1)} %get-tuple-element.15.base_ref, bf16[4,576,128]{2,1,0:T(8,128)(2,1)S(1)} %all-to-all-done.parts_ref), custom_call_target="tpu_custom_call" | custom-call | bytes 2000000 | tf_op jit(solution)/shard_map/scatter/pallas_call | solution.py:305
  16.4 20.8 %all-to-all-start.1 = ((bf16[128,8,128]{2,1,0:T(8,128)(2,1)}), bf16[128,8,128]{2,1,0:T(8,128)(2,1)S(1)}, u32[]{:S(2)}, u32[]{:S(2)}) async-start(bf16[128,8,128]{2,1,0:T(8,128)(2,1)} %bitcast.2), calls=%async_computation.1 | async-start | bytes 524288 | tf_op jit(solution)/shard_map/all_to_all | solution.py:316
  37.1 2.8 %collective-permute-start = (bf16[576,128]{1,0:T(8,128)(2,1)S(1)}, bf16[576,128]{1,0:T(8,128)(2,1)S(1)}, u32[]{:S(2)}, u32[]{:S(2)}) collective-permute-start(bf16[576,128]{1,0:T(8,128)(2,1)S(1)} %get-tuple-element.16.total_ref.own_ref), channel_id=1, source_target_pairs={{0,1},{1,0},{2,3},{3,2},{4,7},{5,6},{6,5},{7,4},{8,9},{9,8},{10,11... | collective-permute-start | bytes 442376 | tf_op jit(solution)/shard_map/ppermute | solution.py:260
  39.9 4.6 %collective-permute-done._.first_ref = bf16[576,128]{1,0:T(8,128)(2,1)S(1)} collective-permute-done((bf16[576,128]{1,0:T(8,128)(2,1)S(1)}, bf16[576,128]{1,0:T(8,128)(2,1)S(1)}, u32[]{:S(2)}, u32[]{:S(2)}) %collective-permute-start) | collective-permute-done | bytes 147488 | tf_op jit(solution)/shard_map/ppermute | solution.py:260
  44.5 7.9 %all-to-all-done.1 = bf16[128,8,128]{2,1,0:T(8,128)(2,1)S(1)} async-done(((bf16[128,8,128]{2,1,0:T(8,128)(2,1)}), bf16[128,8,128]{2,1,0:T(8,128)(2,1)S(1)}, u32[]{:S(2)}, u32[]{:S(2)}) %all-to-all-start.1) | async-done | bytes 262176 | tf_op jit(solution)/shard_map/all_to_all | solution.py:316
  52.4 0.4 compact.1
  52.8 0.0 copy-start.4
  52.8 14.6 %all_to_all.40.pieces_ref = bf16[4,384,256]{2,1,0:T(8,128)(2,1)S(1)} all-to-all(bf16[4,384,256]{2,1,0:T(8,128)(2,1)S(1)} %compact.1), channel_id=1, replica_groups=mesh['fsdp'=128,'rep'=4] {'rep'}, dimensions={0} | all-to-all | bytes 1572864 | tf_op jit(solution)/shard_map/all_to_all | solution.py:265
  67.4 0.0 copy-done.4
  67.4 8.5 %newton_schulz.1 = (bf16[384,1024]{1,0:T(8,128)(2,1)S(1)}, bf16[1024,128]{1,0:T(8,128)(2,1)}, bf16[1152,128]{1,0:T(8,128)(2,1)S(1)}) custom-call(bf16[1024,384]{1,0:T(8,128)(2,1)S(1)} %copy-done.4, bf16[4,384,256]{2,1,0:T(8,128)(2,1)S(1)} %all_to_all.40.pieces_ref, bf16[576,128]{1,0:T(8,128)(2,1)S(1)} %get-tuple-element.16.total_ref.own_ref, ...), custom_call_target="tpu_custom_call" | custom-call | flops 5000000000 | bytes 4000000 | tf_op jit(solution)/shard_map/newton_schulz/pallas_call | solution.py:328
  76.0 6.4 %all-to-all-start.3 = ((bf16[128,8,128]{2,1,0:T(8,128)(2,1)}), bf16[128,8,128]{2,1,0:T(8,128)(2,1)S(1)}, u32[]{:S(2)}, u32[]{:S(2)}) async-start(bf16[128,8,128]{2,1,0:T(8,128)(2,1)} %bitcast.5), calls=%async_computation.3 | async-start | bytes 524288 | tf_op jit(solution)/shard_map/all_to_all | solution.py:347
  82.4 2.2 %collective-permute-start.1 = (bf16[1152,128]{1,0:T(8,128)(2,1)S(1)}, bf16[1152,128]{1,0:T(8,128)(2,1)S(1)}, u32[]{:S(2)}, u32[]{:S(2)}) collective-permute-start(bf16[1152,128]{1,0:T(8,128)(2,1)S(1)} %get-tuple-element.20._), channel_id=1, source_target_pairs={{0,3},{1,2},{2,1},{3,0},{4,5},{5,4},{6,7},{7,6},{8,11},{9,10},{10,... | collective-permute-start | bytes 884744 | tf_op jit(solution)/shard_map/ppermute | solution.py:260
  84.6 0.9 owned.1
  85.5 4.6 %collective-permute-done.1.second_ref = bf16[1152,128]{1,0:T(8,128)(2,1)S(1)} collective-permute-done((bf16[1152,128]{1,0:T(8,128)(2,1)S(1)}, bf16[1152,128]{1,0:T(8,128)(2,1)S(1)}, u32[]{:S(2)}, u32[]{:S(2)}) %collective-permute-start.1) | collective-permute-done | bytes 294944 | tf_op jit(solution)/shard_map/ppermute | solution.py:260
  90.1 2.8 %momentum.1 = (f32[72,4,1024]{2,1,0:T(4,128)}, f32[8,128]{1,0:T(8,128)S(1)}) custom-call(s32[72,128]{1,0:T(8,128)S(1)} %copy-done.1, f32[72,4,1024]{2,1,0:T(4,128)S(1)} %bitcast.10, bf16[576,128]{1,0:T(8,128)(2,1)S(1)} %get-tuple-element.16.total_ref.own_ref, bf16[576,128]{1,0:T(8,128)(2,1)S(1)} %collective-permute-done._.first_ref, ...), custom_call_target="tpu_custom_call" | custom-call | bytes 4000000 | tf_op jit(solution)/shard_map/momentum/pallas_call | solution.py:348
  92.9 4.8 %all-to-all-done.3 = bf16[128,8,128]{2,1,0:T(8,128)(2,1)S(1)} async-done(((bf16[128,8,128]{2,1,0:T(8,128)(2,1)}), bf16[128,8,128]{2,1,0:T(8,128)(2,1)S(1)}, u32[]{:S(2)}, u32[]{:S(2)}) %all-to-all-start.3) | async-done | bytes 262176 | tf_op jit(solution)/shard_map/all_to_all | solution.py:347
  97.7 0.6 select.1
  98.3 12.0 %all_to_all.41.pieces_ref = bf16[4,576,128]{2,1,0:T(8,128)(2,1)S(1)} all-to-all(bf16[4,576,128]{2,1,0:T(8,128)(2,1)S(1)} %select.1), channel_id=1, replica_groups=mesh['fsdp'=128,'rep'=4] {'rep'}, dimensions={0} | all-to-all | bytes 1179648 | tf_op jit(solution)/shard_map/all_to_all | solution.py:265
  110.4 1.0 update.1
Async XLA Ops:
  0.6 7.0 %copy-start = (f32[1,72,4,1024]{3,2,1,0:T(4,128)S(1)}, f32[1,72,4,1024]{3,2,1,0:T(4,128)}, u32[]{:S(2)}) copy-start(f32[1,72,4,1024]{3,2,1,0:T(4,128)} %param.5) | copy-start | bytes 3538948
  0.6 7.0 %copy-start.1 = (s32[72,128]{1,0:T(8,128)S(1)}, s32[72,128]{1,0:T(8,128)}, u32[]{:S(2)}) copy-start(s32[72,128]{1,0:T(8,128)} %lens_ref.3) | copy-start | bytes 110596
  0.7 7.0 %copy-start.2 = (s32[72]{0:T(128)S(1)}, s32[72]{0:T(128)}, u32[]{:S(2)}) copy-start(s32[72]{0:T(128)} %owner_ref.5) | copy-start | bytes 868
  2.8 12.1 %all-to-all-start = ((bf16[4,576,128]{2,1,0:T(8,128)(2,1)}), bf16[4,576,128]{2,1,0:T(8,128)(2,1)S(1)}, u32[]{:S(2)}, u32[]{:S(2)}) async-start(bf16[4,576,128]{2,1,0:T(8,128)(2,1)} %split.1), calls=%async_computation | async-start | bytes 1179648 | tf_op jit(solution)/shard_map/all_to_all | solution.py:265
  10.0 0.9 copy-start.3
  16.4 36.0 %all-to-all-start.1 = ((bf16[128,8,128]{2,1,0:T(8,128)(2,1)}), bf16[128,8,128]{2,1,0:T(8,128)(2,1)S(1)}, u32[]{:S(2)}, u32[]{:S(2)}) async-start(bf16[128,8,128]{2,1,0:T(8,128)(2,1)} %bitcast.2), calls=%async_computation.1 | async-start | bytes 524288 | tf_op jit(solution)/shard_map/all_to_all | solution.py:316
  37.1 7.4 %collective-permute-start = (bf16[576,128]{1,0:T(8,128)(2,1)S(1)}, bf16[576,128]{1,0:T(8,128)(2,1)S(1)}, u32[]{:S(2)}, u32[]{:S(2)}) collective-permute-start(bf16[576,128]{1,0:T(8,128)(2,1)S(1)} %get-tuple-element.16.total_ref.own_ref), channel_id=1, source_target_pairs={{0,1},{1,0},{2,3},{3,2},{4,7},{5,6},{6,5},{7,4},{8,9},{9,8},{10,11... | collective-permute-start | bytes 442376 | tf_op jit(solution)/shard_map/ppermute | solution.py:260
  52.8 14.6 %copy-start.4 = (bf16[1024,384]{1,0:T(8,128)(2,1)S(1)}, bf16[1024,384]{1,0:T(8,128)(2,1)}, u32[]{:S(2)}) copy-start(bf16[1024,384]{1,0:T(8,128)(2,1)} %copy-done.3) | copy-start | bytes 2359300
  76.0 21.7 %all-to-all-start.3 = ((bf16[128,8,128]{2,1,0:T(8,128)(2,1)}), bf16[128,8,128]{2,1,0:T(8,128)(2,1)S(1)}, u32[]{:S(2)}, u32[]{:S(2)}) async-start(bf16[128,8,128]{2,1,0:T(8,128)(2,1)} %bitcast.5), calls=%async_computation.3 | async-start | bytes 524288 | tf_op jit(solution)/shard_map/all_to_all | solution.py:347
  82.4 7.8 %collective-permute-start.1 = (bf16[1152,128]{1,0:T(8,128)(2,1)S(1)}, bf16[1152,128]{1,0:T(8,128)(2,1)S(1)}, u32[]{:S(2)}, u32[]{:S(2)}) collective-permute-start(bf16[1152,128]{1,0:T(8,128)(2,1)S(1)} %get-tuple-element.20._), channel_id=1, source_target_pairs={{0,3},{1,2},{2,1},{3,0},{4,5},{5,4},{6,7},{7,6},{8,11},{9,10},{10,... | collective-permute-start | bytes 884744 | tf_op jit(solution)/shard_map/ppermute | solution.py:260

commit v4 on v3

--- a/solution.py
+++ b/solution.py
@@ -17,6 +17,7 @@
 
 LANES = 128
 ROWS = 8
+UPDATE_PARTS = 3
 BF16 = jnp.bfloat16
 F32 = jnp.float32
 VMEM_LIMIT = 24 * 1024 * 1024
@@ -174,19 +175,21 @@
         square = jnp.dot(gram, gram, preferred_element_type=F32)
         return (COEF_B * gram.astype(F32) + COEF_C * square).astype(BF16)
 
+    pairs = [slice(at, at + 2 * wide) for at in range(0, blocks * wide, 2 * wide)]
+
     def next_of(poly, tile):
         part = x[:, tile]
         return (COEF_A * part.astype(F32) + jnp.dot(poly, part, preferred_element_type=F32)).astype(BF16)
 
     def step(index, carry):
         poly = poly_of()
-        for tile in tiles:
+        for tile in pairs:
             x[:, tile] = next_of(poly, tile)
         return carry
 
     lax.fori_loop(0, ITERS - 1, step, 0)
     poly = poly_of()
-    for tile in tiles:
+    for tile in pairs:
         scaled_ref[:, tile] = (-scale * next_of(poly, tile).astype(F32)).astype(BF16)
     mine = scaled_ref[:, pl.ds(column_of(0, lax.axis_index("rep")), wide)]
     upper = in_half((place_ref.shape[0], LANES), 0)
@@ -234,9 +237,20 @@
             yield pl.ds(column_of(half, block), LANES), got[:, half * slots:(half + 1) * slots, :]
 
 
-def update_kernel(pieces_ref, out_ref):
-    for at, got in columns([(block, pieces_ref.at[block]) for block in range(pieces_ref.shape[0])], out_ref.shape[0]):
-        out_ref[:, :, at] = got.astype(BF16)
+def update_kernel(pieces_ref, out_ref, made, sems):
+    count = made.shape[0]
+    some = count // UPDATE_PARTS
+    copies = []
+    for at in range(0, count, some):
+        blocks = [
+            (block, pieces_ref.at[block, at * ROWS:(at + some) * ROWS, :]) for block in range(pieces_ref.shape[0])
+        ]
+        for lanes, got in columns(blocks, some):
+            made[at:at + some, :, lanes] = got.astype(BF16)
+        copies.append(pltpu.make_async_copy(made.at[at:at + some], out_ref.at[at:at + some], sems.at[len(copies)]))
+        copies[-1].start()
+    for copy in copies:
+        copy.wait()
 
 
 def momentum_kernel(lens_ref, mom_ref, own_ref, first_ref, second_ref, _, out_ref, done_ref, total):
@@ -369,7 +383,8 @@
         update_kernel,
         out_shape=shape((count, slots, width), BF16),
         in_specs=[vmem()],
-        out_specs=vmem(),
+        out_specs=hbm(),
+        scratch_shapes=[pltpu.VMEM((count, slots, width), BF16), pltpu.SemaphoreType.DMA((UPDATE_PARTS,))],
         compiler_params=params(),
         cost_estimate=cost(0, 2_000_000),
         name="update",

time: 112 us -> 112 us (level)
  no operation moved by 1% of the time
where the time goes in v4:
time: 112 us; the launch traced here: 111 us
  starting transfers between devices  37 us (33%)
  blocking collectives  26.6 us (24%)
  waiting for transfers between devices  25.9 us (23%)
  Pallas kernels  20 us (18%)
    all_to_all x2, blocking collectives, exchange(): lax.all_to_all(flat, 'rep', split_axis=0, concat_axis=0, tiled=True)  26.6 us
    all_to_all x1, starting transfers between devices, body(): lax.all_to_all(send, 'fsdp', split_axis=0, concat_axis=0, tiled=True)  20.8 us
    ppermute x2, waiting for transfers between devices, swap(): return lax.ppermute(value, ('fsdp', 'rep'), pairs)  9.21 us
    pallas_call x1, Pallas kernels, body(): pl.pallas_call(functools.partial(newton_schulz_kernel, math.sqrt(max(R, w...  8.55 us
    all_to_all x1, waiting for transfers between devices, body(): lax.all_to_all(send, 'fsdp', split_axis=0, concat_axis=0, tiled=True)  7.86 us
    all_to_all x1, starting transfers between devices, body(): lax.all_to_all(back, 'fsdp', split_axis=0, concat_axis=0, tiled=True)  6.41 us
    ppermute x2, starting transfers between devices, swap(): return lax.ppermute(value, ('fsdp', 'rep'), pairs)  5 us
    all_to_all x1, starting transfers between devices, exchange(): lax.all_to_all(flat, 'rep', split_axis=0, concat_axis=0, tiled=True)  4.85 us
  transfers between devices with their start and end apart: 5, of which 5 were waited for; matrix products, arithmetic and copies ran while one was open for 0% of the time, Pallas kernels for 5%

profile of v4, /device:TPU:1, one launch (start us, length us, event | category | flops | bytes accessed | tf_op | source)
XLA Modules:
  0.0 111.2 jit_solution(3956247903497889386)
XLA Ops:
  0.6 0.0 copy-start
  0.6 0.0 copy-start.1
  0.7 0.0 copy-start.2
  0.7 2.1 %split.1 = bf16[4,576,128]{2,1,0:T(8,128)(2,1)} custom-call(f32[72,4,1024]{2,1,0:T(4,128)} %bitcast.13), custom_call_target="tpu_custom_call" | custom-call | bytes 2000000 | tf_op jit(solution)/shard_map/split/pallas_call | solution.py:292
  2.8 4.9 %all-to-all-start = ((bf16[4,576,128]{2,1,0:T(8,128)(2,1)}), bf16[4,576,128]{2,1,0:T(8,128)(2,1)S(1)}, u32[]{:S(2)}, u32[]{:S(2)}) async-start(bf16[4,576,128]{2,1,0:T(8,128)(2,1)} %split.1), calls=%async_computation | async-start | bytes 1179648 | tf_op jit(solution)/shard_map/all_to_all | solution.py:279
  7.6 0.0 copy-done
  7.6 0.0 copy-done.1
  7.6 0.0 copy-done.2
  7.6 2.3 %own.1 = (f32[576,128]{1,0:T(8,128)S(1)}, bf16[384,1024]{1,0:T(8,128)(2,1)S(1)}, bf16[1024,384]{1,0:T(8,128)(2,1)S(1)}) custom-call(s32[72]{0:T(128)S(1)} %copy-done.2, s32[72,128]{1,0:T(8,128)S(1)} %copy-done.1, f32[72,4,1024]{2,1,0:T(4,128)S(1)} %bitcast.9), custom_call_target="tpu_custom_call" | custom-call | bytes 4000000 | tf_op jit(solution)/shard_map/own/pallas_call | solution.py:309
  10.0 0.0 copy-start.3
  10.0 0.9 copy-done.3
  10.8 4.1 %all-to-all-done.parts_ref = bf16[4,576,128]{2,1,0:T(8,128)(2,1)S(1)} async-done(((bf16[4,576,128]{2,1,0:T(8,128)(2,1)}), bf16[4,576,128]{2,1,0:T(8,128)(2,1)S(1)}, u32[]{:S(2)}, u32[]{:S(2)}) %all-to-all-start) | async-done | bytes 589856 | tf_op jit(solution)/shard_map/all_to_all | solution.py:279
  14.9 1.5 %scatter.1 = (bf16[1024,128]{1,0:T(8,128)(2,1)}, bf16[576,128]{1,0:T(8,128)(2,1)S(1)}) custom-call(s32[72]{0:T(128)S(1)} %copy-done.2, f32[576,128]{1,0:T(8,128)S(1)} %get-tuple-element.15.base_ref, bf16[4,576,128]{2,1,0:T(8,128)(2,1)S(1)} %all-to-all-done.parts_ref), custom_call_target="tpu_custom_call" | custom-call | bytes 2000000 | tf_op jit(solution)/shard_map/scatter/pallas_call | solution.py:319
  16.4 20.8 %all-to-all-start.1 = ((bf16[128,8,128]{2,1,0:T(8,128)(2,1)}), bf16[128,8,128]{2,1,0:T(8,128)(2,1)S(1)}, u32[]{:S(2)}, u32[]{:S(2)}) async-start(bf16[128,8,128]{2,1,0:T(8,128)(2,1)} %bitcast.2), calls=%async_computation.1 | async-start | bytes 524288 | tf_op jit(solution)/shard_map/all_to_all | solution.py:330
  37.1 2.8 %collective-permute-start = (bf16[576,128]{1,0:T(8,128)(2,1)S(1)}, bf16[576,128]{1,0:T(8,128)(2,1)S(1)}, u32[]{:S(2)}, u32[]{:S(2)}) collective-permute-start(bf16[576,128]{1,0:T(8,128)(2,1)S(1)} %get-tuple-element.16.total_ref.own_ref), channel_id=1, source_target_pairs={{0,1},{1,0},{2,3},{3,2},{4,7},{5,6},{6,5},{7,4},{8,9},{9,8},{10,11... | collective-permute-start | bytes 442376 | tf_op jit(solution)/shard_map/ppermute | solution.py:274
  39.9 4.6 %collective-permute-done._.first_ref = bf16[576,128]{1,0:T(8,128)(2,1)S(1)} collective-permute-done((bf16[576,128]{1,0:T(8,128)(2,1)S(1)}, bf16[576,128]{1,0:T(8,128)(2,1)S(1)}, u32[]{:S(2)}, u32[]{:S(2)}) %collective-permute-start) | collective-permute-done | bytes 147488 | tf_op jit(solution)/shard_map/ppermute | solution.py:274
  44.5 7.9 %all-to-all-done.1 = bf16[128,8,128]{2,1,0:T(8,128)(2,1)S(1)} async-done(((bf16[128,8,128]{2,1,0:T(8,128)(2,1)}), bf16[128,8,128]{2,1,0:T(8,128)(2,1)S(1)}, u32[]{:S(2)}, u32[]{:S(2)}) %all-to-all-start.1) | async-done | bytes 262176 | tf_op jit(solution)/shard_map/all_to_all | solution.py:330
  52.4 0.4 compact.1
  52.8 0.0 copy-start.4
  52.8 14.6 %all_to_all.40.pieces_ref = bf16[4,384,256]{2,1,0:T(8,128)(2,1)S(1)} all-to-all(bf16[4,384,256]{2,1,0:T(8,128)(2,1)S(1)} %compact.1), channel_id=1, replica_groups=mesh['fsdp'=128,'rep'=4] {'rep'}, dimensions={0} | all-to-all | bytes 1572864 | tf_op jit(solution)/shard_map/all_to_all | solution.py:279
  67.4 0.0 copy-done.4
  67.4 8.6 %newton_schulz.1 = (bf16[384,1024]{1,0:T(8,128)(2,1)S(1)}, bf16[1024,128]{1,0:T(8,128)(2,1)}, bf16[1152,128]{1,0:T(8,128)(2,1)S(1)}) custom-call(bf16[1024,384]{1,0:T(8,128)(2,1)S(1)} %copy-done.4, bf16[4,384,256]{2,1,0:T(8,128)(2,1)S(1)} %all_to_all.40.pieces_ref, bf16[576,128]{1,0:T(8,128)(2,1)S(1)} %get-tuple-element.16.total_ref.own_ref, ...), custom_call_target="tpu_custom_call" | custom-call | flops 5000000000 | bytes 4000000 | tf_op jit(solution)/shard_map/newton_schulz/pallas_call | solution.py:342
  76.0 6.4 %all-to-all-start.3 = ((bf16[128,8,128]{2,1,0:T(8,128)(2,1)}), bf16[128,8,128]{2,1,0:T(8,128)(2,1)S(1)}, u32[]{:S(2)}, u32[]{:S(2)}) async-start(bf16[128,8,128]{2,1,0:T(8,128)(2,1)} %bitcast.5), calls=%async_computation.3 | async-start | bytes 524288 | tf_op jit(solution)/shard_map/all_to_all | solution.py:361
  82.4 2.2 %collective-permute-start.1 = (bf16[1152,128]{1,0:T(8,128)(2,1)S(1)}, bf16[1152,128]{1,0:T(8,128)(2,1)S(1)}, u32[]{:S(2)}, u32[]{:S(2)}) collective-permute-start(bf16[1152,128]{1,0:T(8,128)(2,1)S(1)} %get-tuple-element.20._), channel_id=1, source_target_pairs={{0,3},{1,2},{2,1},{3,0},{4,5},{5,4},{6,7},{7,6},{8,11},{9,10},{10,... | collective-permute-start | bytes 884744 | tf_op jit(solution)/shard_map/ppermute | solution.py:274
  84.6 0.9 owned.1
  85.5 4.6 %collective-permute-done.1.second_ref = bf16[1152,128]{1,0:T(8,128)(2,1)S(1)} collective-permute-done((bf16[1152,128]{1,0:T(8,128)(2,1)S(1)}, bf16[1152,128]{1,0:T(8,128)(2,1)S(1)}, u32[]{:S(2)}, u32[]{:S(2)}) %collective-permute-start.1) | collective-permute-done | bytes 294944 | tf_op jit(solution)/shard_map/ppermute | solution.py:274
  90.1 2.8 %momentum.1 = (f32[72,4,1024]{2,1,0:T(4,128)}, f32[8,128]{1,0:T(8,128)S(1)}) custom-call(s32[72,128]{1,0:T(8,128)S(1)} %copy-done.1, f32[72,4,1024]{2,1,0:T(4,128)S(1)} %bitcast.10, bf16[576,128]{1,0:T(8,128)(2,1)S(1)} %get-tuple-element.16.total_ref.own_ref, bf16[576,128]{1,0:T(8,128)(2,1)S(1)} %collective-permute-done._.first_ref, ...), custom_call_target="tpu_custom_call" | custom-call | bytes 4000000 | tf_op jit(solution)/shard_map/momentum/pallas_call | solution.py:362
  92.9 4.8 %all-to-all-done.3 = bf16[128,8,128]{2,1,0:T(8,128)(2,1)S(1)} async-done(((bf16[128,8,128]{2,1,0:T(8,128)(2,1)}), bf16[128,8,128]{2,1,0:T(8,128)(2,1)S(1)}, u32[]{:S(2)}, u32[]{:S(2)}) %all-to-all-start.3) | async-done | bytes 262176 | tf_op jit(solution)/shard_map/all_to_all | solution.py:361
  97.7 0.6 select.1
  98.3 12.0 %all_to_all.41.pieces_ref = bf16[4,576,128]{2,1,0:T(8,128)(2,1)S(1)} all-to-all(bf16[4,576,128]{2,1,0:T(8,128)(2,1)S(1)} %select.1), channel_id=1, replica_groups=mesh['fsdp'=128,'rep'=4] {'rep'}, dimensions={0} | all-to-all | bytes 1179648 | tf_op jit(solution)/shard_map/all_to_all | solution.py:279
  110.4 0.9 update.1
Async XLA Ops:
  0.6 7.0 %copy-start = (f32[1,72,4,1024]{3,2,1,0:T(4,128)S(1)}, f32[1,72,4,1024]{3,2,1,0:T(4,128)}, u32[]{:S(2)}) copy-start(f32[1,72,4,1024]{3,2,1,0:T(4,128)} %param.5) | copy-start | bytes 3538948
  0.6 7.0 %copy-start.1 = (s32[72,128]{1,0:T(8,128)S(1)}, s32[72,128]{1,0:T(8,128)}, u32[]{:S(2)}) copy-start(s32[72,128]{1,0:T(8,128)} %lens_ref.3) | copy-start | bytes 110596
  0.7 7.0 %copy-start.2 = (s32[72]{0:T(128)S(1)}, s32[72]{0:T(128)}, u32[]{:S(2)}) copy-start(s32[72]{0:T(128)} %owner_ref.5) | copy-start | bytes 868
  2.8 12.1 %all-to-all-start = ((bf16[4,576,128]{2,1,0:T(8,128)(2,1)}), bf16[4,576,128]{2,1,0:T(8,128)(2,1)S(1)}, u32[]{:S(2)}, u32[]{:S(2)}) async-start(bf16[4,576,128]{2,1,0:T(8,128)(2,1)} %split.1), calls=%async_computation | async-start | bytes 1179648 | tf_op jit(solution)/shard_map/all_to_all | solution.py:279
  10.0 0.9 copy-start.3
  16.4 36.0 %all-to-all-start.1 = ((bf16[128,8,128]{2,1,0:T(8,128)(2,1)}), bf16[128,8,128]{2,1,0:T(8,128)(2,1)S(1)}, u32[]{:S(2)}, u32[]{:S(2)}) async-start(bf16[128,8,128]{2,1,0:T(8,128)(2,1)} %bitcast.2), calls=%async_computation.1 | async-start | bytes 524288 | tf_op jit(solution)/shard_map/all_to_all | solution.py:330
  37.1 7.4 %collective-permute-start = (bf16[576,128]{1,0:T(8,128)(2,1)S(1)}, bf16[576,128]{1,0:T(8,128)(2,1)S(1)}, u32[]{:S(2)}, u32[]{:S(2)}) collective-permute-start(bf16[576,128]{1,0:T(8,128)(2,1)S(1)} %get-tuple-element.16.total_ref.own_ref), channel_id=1, source_target_pairs={{0,1},{1,0},{2,3},{3,2},{4,7},{5,6},{6,5},{7,4},{8,9},{9,8},{10,11... | collective-permute-start | bytes 442376 | tf_op jit(solution)/shard_map/ppermute | solution.py:274
  52.8 14.6 %copy-start.4 = (bf16[1024,384]{1,0:T(8,128)(2,1)S(1)}, bf16[1024,384]{1,0:T(8,128)(2,1)}, u32[]{:S(2)}) copy-start(bf16[1024,384]{1,0:T(8,128)(2,1)} %copy-done.3) | copy-start | bytes 2359300
  76.0 21.7 %all-to-all-start.3 = ((bf16[128,8,128]{2,1,0:T(8,128)(2,1)}), bf16[128,8,128]{2,1,0:T(8,128)(2,1)S(1)}, u32[]{:S(2)}, u32[]{:S(2)}) async-start(bf16[128,8,128]{2,1,0:T(8,128)(2,1)} %bitcast.5), calls=%async_computation.3 | async-start | bytes 524288 | tf_op jit(solution)/shard_map/all_to_all | solution.py:361
  82.4 7.8 %collective-permute-start.1 = (bf16[1152,128]{1,0:T(8,128)(2,1)S(1)}, bf16[1152,128]{1,0:T(8,128)(2,1)S(1)}, u32[]{:S(2)}, u32[]{:S(2)}) collective-permute-start(bf16[1152,128]{1,0:T(8,128)(2,1)S(1)} %get-tuple-element.20._), channel_id=1, source_target_pairs={{0,3},{1,2},{2,1},{3,0},{4,5},{5,4},{6,7},{7,6},{8,11},{9,10},{10,... | collective-permute-start | bytes 884744 | tf_op jit(solution)/shard_map/ppermute | solution.py:274

commit v5 on v4

--- a/solution.py
+++ b/solution.py
@@ -59,6 +59,19 @@
     for half in range(2):
         scratch[:, half * slots:(half + 1) * slots, :] = src_ref[:, :, pl.ds(column_of(half, block), LANES)]
     return scratch[...].reshape(scratch.shape[0] * ROWS, LANES)
+
+
+def write_out(rows_of, made, out_ref, sems):
+    parts = sems.shape[0]
+    some = made.shape[0] // parts
+    copies = []
+    for part in range(parts):
+        at = slice(part * some, (part + 1) * some)
+        made[at, :] = rows_of(at)
+        copies.append(pltpu.make_async_copy(made.at[at], out_ref.at[at], sems.at[part]))
+        copies[-1].start()
+    for copy in copies:
+        copy.wait()
 
 
 def split_kernel(g_ref, out_ref, arrived, scratch, packed, in_sems, out_sems):
@@ -84,7 +97,7 @@
     pick_kernel(owner_ref, lens_ref, pick_ref, place_ref)
 
 
-def scatter_kernel(owner_ref, base_ref, parts_ref, send_ref, tot_ref, packed):
+def scatter_kernel(owner_ref, base_ref, parts_ref, send_ref, tot_ref, packed, rounded, sems):
     reps = parts_ref.shape[0]
     total = parts_ref[0].astype(F32)
     for rep in range(1, reps):
@@ -95,7 +108,7 @@
     for m in range(nm.shape[0] // ROWS):
         at = pl.multiple_of(owner_ref[m] * ROWS, ROWS)
         packed[pl.ds(at, ROWS), :] = nm[m * ROWS:(m + 1) * ROWS, :]
-    send_ref[...] = packed[...].astype(BF16)
+    write_out(lambda at: packed[at, :].astype(BF16), rounded, send_ref, sems)
 
 
 def pick_kernel(owner_ref, lens_ref, pick_ref, place_ref):
@@ -152,7 +165,7 @@
         out_ref[rep] = picked
 
 
-def newton_schulz_kernel(scale, place_ref, pieces_ref, total_ref, first_ref, scaled_ref, back_ref, joined_ref, x):
+def newton_schulz_kernel(scale, place_ref, pieces_ref, total_ref, first_ref, scaled_ref, back_ref, joined_ref, x, made, sems):
     rows8 = total_ref.shape[0]
     joined_ref[:rows8, :] = total_ref[...]
     joined_ref[rows8:, :] = first_ref[...]
@@ -192,9 +205,13 @@
     for tile in pairs:
         scaled_ref[:, tile] = (-scale * next_of(poly, tile).astype(F32)).astype(BF16)
     mine = scaled_ref[:, pl.ds(column_of(0, lax.axis_index("rep")), wide)]
-    upper = in_half((place_ref.shape[0], LANES), 0)
-    spread = jnp.dot(place_ref[...], mine, preferred_element_type=F32)
-    back_ref[...] = jnp.where(upper, spread[:, :LANES], spread[:, LANES:]).astype(BF16)
+    upper = in_half((place_ref.shape[0] // sems.shape[0], LANES), 0)
+
+    def rows_of(at):
+        spread = jnp.dot(place_ref[at, :], mine, preferred_element_type=F32)
+        return jnp.where(upper, spread[:, :LANES], spread[:, LANES:]).astype(BF16)
+
+    write_out(rows_of, made, back_ref, sems)
 
 
 def owned_kernel(scaled_ref, _, owned_ref, done_ref):
@@ -320,8 +337,12 @@
         scatter_kernel,
         out_shape=[shape((slots8, LANES), BF16), part],
         in_specs=[smem(), vmem(), vmem()],
-        out_specs=[vmem()] * 2,
-        scratch_shapes=[pltpu.VMEM((slots8, LANES), F32)],
+        out_specs=[hbm(), vmem()],
+        scratch_shapes=[
+            pltpu.VMEM((slots8, LANES), F32),
+            pltpu.VMEM((slots8, LANES), BF16),
+            pltpu.SemaphoreType.DMA((4,)),
+        ],
         compiler_params=params(),
         cost_estimate=cost(0, 2_000_000),
         name="scatter",
@@ -343,8 +364,12 @@
         functools.partial(newton_schulz_kernel, math.sqrt(max(R, width))),
         out_shape=[shape((R, width), BF16), shape((slots8, LANES), BF16), shape((2 * rows8, LANES), BF16)],
         in_specs=[vmem()] * 4,
-        out_specs=[vmem()] * 3,
-        scratch_shapes=[pltpu.VMEM((R, width), BF16)],
+        out_specs=[vmem(), hbm(), vmem()],
+        scratch_shapes=[
+            pltpu.VMEM((R, width), BF16),
+            pltpu.VMEM((slots8, LANES), BF16),
+            pltpu.SemaphoreType.DMA((4,)),
+        ],
         compiler_params=params(),
         cost_estimate=cost(5_000_000_000, 4_000_000),
         name="newton_schulz",

time: 112 us -> 112 us (level)
  no operation moved by 1% of the time
where the time goes in v5:
time: 112 us; the launch traced here: 111 us
  starting transfers between devices  37.1 us (33%)
  blocking collectives  26.6 us (24%)
  waiting for transfers between devices  26 us (23%)
  Pallas kernels  20 us (18%)
    all_to_all x2, blocking collectives, exchange(): lax.all_to_all(flat, 'rep', split_axis=0, concat_axis=0, tiled=True)  26.6 us
    all_to_all x1, starting transfers between devices, body(): lax.all_to_all(send, 'fsdp', split_axis=0, concat_axis=0, tiled=True)  20.8 us
    ppermute x2, waiting for transfers between devices, swap(): return lax.ppermute(value, ('fsdp', 'rep'), pairs)  9.21 us
    pallas_call x1, Pallas kernels, body(): pl.pallas_call(functools.partial(newton_schulz_kernel, math.sqrt(max(R, w...  8.5 us
    all_to_all x1, waiting for transfers between devices, body(): lax.all_to_all(send, 'fsdp', split_axis=0, concat_axis=0, tiled=True)  7.86 us
    all_to_all x1, starting transfers between devices, body(): lax.all_to_all(back, 'fsdp', split_axis=0, concat_axis=0, tiled=True)  6.43 us
    ppermute x2, starting transfers between devices, swap(): return lax.ppermute(value, ('fsdp', 'rep'), pairs)  5 us
    all_to_all x1, starting transfers between devices, exchange(): lax.all_to_all(flat, 'rep', split_axis=0, concat_axis=0, tiled=True)  4.85 us
  transfers between devices with their start and end apart: 5, of which 5 were waited for; matrix products, arithmetic and copies ran while one was open for 0% of the time, Pallas kernels for 5%

profile of v5, /device:TPU:1, one launch (start us, length us, event | category | flops | bytes accessed | tf_op | source)
XLA Modules:
  0.0 111.3 jit_solution(1156736157511216087)
XLA Ops:
  0.6 0.0 copy-start
  0.6 0.0 copy-start.1
  0.7 0.0 copy-start.2
  0.7 2.1 %split.1 = bf16[4,576,128]{2,1,0:T(8,128)(2,1)} custom-call(f32[72,4,1024]{2,1,0:T(4,128)} %bitcast.13), custom_call_target="tpu_custom_call" | custom-call | bytes 2000000 | tf_op jit(solution)/shard_map/split/pallas_call | solution.py:309
  2.8 4.9 %all-to-all-start = ((bf16[4,576,128]{2,1,0:T(8,128)(2,1)}), bf16[4,576,128]{2,1,0:T(8,128)(2,1)S(1)}, u32[]{:S(2)}, u32[]{:S(2)}) async-start(bf16[4,576,128]{2,1,0:T(8,128)(2,1)} %split.1), calls=%async_computation | async-start | bytes 1179648 | tf_op jit(solution)/shard_map/all_to_all | solution.py:296
  7.6 0.0 copy-done
  7.6 0.0 copy-done.1
  7.6 0.0 copy-done.2
  7.6 2.3 %own.1 = (f32[576,128]{1,0:T(8,128)S(1)}, bf16[384,1024]{1,0:T(8,128)(2,1)S(1)}, bf16[1024,384]{1,0:T(8,128)(2,1)S(1)}) custom-call(s32[72]{0:T(128)S(1)} %copy-done.2, s32[72,128]{1,0:T(8,128)S(1)} %copy-done.1, f32[72,4,1024]{2,1,0:T(4,128)S(1)} %bitcast.9), custom_call_target="tpu_custom_call" | custom-call | bytes 4000000 | tf_op jit(solution)/shard_map/own/pallas_call | solution.py:326
  10.0 0.0 copy-start.3
  10.0 0.9 copy-done.3
  10.8 4.1 %all-to-all-done.parts_ref = bf16[4,576,128]{2,1,0:T(8,128)(2,1)S(1)} async-done(((bf16[4,576,128]{2,1,0:T(8,128)(2,1)}), bf16[4,576,128]{2,1,0:T(8,128)(2,1)S(1)}, u32[]{:S(2)}, u32[]{:S(2)}) %all-to-all-start) | async-done | bytes 589856 | tf_op jit(solution)/shard_map/all_to_all | solution.py:296
  14.9 1.5 %scatter.1 = (bf16[1024,128]{1,0:T(8,128)(2,1)}, bf16[576,128]{1,0:T(8,128)(2,1)S(1)}) custom-call(s32[72]{0:T(128)S(1)} %copy-done.2, f32[576,128]{1,0:T(8,128)S(1)} %get-tuple-element.15.base_ref, bf16[4,576,128]{2,1,0:T(8,128)(2,1)S(1)} %all-to-all-done.parts_ref), custom_call_target="tpu_custom_call" | custom-call | bytes 2000000 | tf_op jit(solution)/shard_map/scatter/pallas_call | solution.py:336
  16.4 20.8 %all-to-all-start.1 = ((bf16[128,8,128]{2,1,0:T(8,128)(2,1)}), bf16[128,8,128]{2,1,0:T(8,128)(2,1)S(1)}, u32[]{:S(2)}, u32[]{:S(2)}) async-start(bf16[128,8,128]{2,1,0:T(8,128)(2,1)} %bitcast.2), calls=%async_computation.1 | async-start | bytes 524288 | tf_op jit(solution)/shard_map/all_to_all | solution.py:351
  37.2 2.8 %collective-permute-start = (bf16[576,128]{1,0:T(8,128)(2,1)S(1)}, bf16[576,128]{1,0:T(8,128)(2,1)S(1)}, u32[]{:S(2)}, u32[]{:S(2)}) collective-permute-start(bf16[576,128]{1,0:T(8,128)(2,1)S(1)} %get-tuple-element.16.total_ref.own_ref), channel_id=1, source_target_pairs={{0,1},{1,0},{2,3},{3,2},{4,7},{5,6},{6,5},{7,4},{8,9},{9,8},{10,11... | collective-permute-start | bytes 442376 | tf_op jit(solution)/shard_map/ppermute | solution.py:291
  40.0 4.6 %collective-permute-done._.first_ref = bf16[576,128]{1,0:T(8,128)(2,1)S(1)} collective-permute-done((bf16[576,128]{1,0:T(8,128)(2,1)S(1)}, bf16[576,128]{1,0:T(8,128)(2,1)S(1)}, u32[]{:S(2)}, u32[]{:S(2)}) %collective-permute-start) | collective-permute-done | bytes 147488 | tf_op jit(solution)/shard_map/ppermute | solution.py:291
  44.6 7.9 %all-to-all-done.1 = bf16[128,8,128]{2,1,0:T(8,128)(2,1)S(1)} async-done(((bf16[128,8,128]{2,1,0:T(8,128)(2,1)}), bf16[128,8,128]{2,1,0:T(8,128)(2,1)S(1)}, u32[]{:S(2)}, u32[]{:S(2)}) %all-to-all-start.1) | async-done | bytes 262176 | tf_op jit(solution)/shard_map/all_to_all | solution.py:351
  52.4 0.4 compact.1
  52.8 0.0 copy-start.4
  52.9 14.6 %all_to_all.40.pieces_ref = bf16[4,384,256]{2,1,0:T(8,128)(2,1)S(1)} all-to-all(bf16[4,384,256]{2,1,0:T(8,128)(2,1)S(1)} %compact.1), channel_id=1, replica_groups=mesh['fsdp'=128,'rep'=4] {'rep'}, dimensions={0} | all-to-all | bytes 1572864 | tf_op jit(solution)/shard_map/all_to_all | solution.py:296
  67.4 0.0 copy-done.4
  67.4 8.5 %newton_schulz.1 = (bf16[384,1024]{1,0:T(8,128)(2,1)S(1)}, bf16[1024,128]{1,0:T(8,128)(2,1)}, bf16[1152,128]{1,0:T(8,128)(2,1)S(1)}) custom-call(bf16[1024,384]{1,0:T(8,128)(2,1)S(1)} %copy-done.4, bf16[4,384,256]{2,1,0:T(8,128)(2,1)S(1)} %all_to_all.40.pieces_ref, bf16[576,128]{1,0:T(8,128)(2,1)S(1)} %get-tuple-element.16.total_ref.own_ref, ...), custom_call_target="tpu_custom_call" | custom-call | flops 5000000000 | bytes 4000000 | tf_op jit(solution)/shard_map/newton_schulz/pallas_call | solution.py:363
  75.9 6.4 %all-to-all-start.3 = ((bf16[128,8,128]{2,1,0:T(8,128)(2,1)}), bf16[128,8,128]{2,1,0:T(8,128)(2,1)S(1)}, u32[]{:S(2)}, u32[]{:S(2)}) async-start(bf16[128,8,128]{2,1,0:T(8,128)(2,1)} %bitcast.5), calls=%async_computation.3 | async-start | bytes 524288 | tf_op jit(solution)/shard_map/all_to_all | solution.py:386
  82.4 2.2 %collective-permute-start.1 = (bf16[1152,128]{1,0:T(8,128)(2,1)S(1)}, bf16[1152,128]{1,0:T(8,128)(2,1)S(1)}, u32[]{:S(2)}, u32[]{:S(2)}) collective-permute-start(bf16[1152,128]{1,0:T(8,128)(2,1)S(1)} %get-tuple-element.20._), channel_id=1, source_target_pairs={{0,3},{1,2},{2,1},{3,0},{4,5},{5,4},{6,7},{7,6},{8,11},{9,10},{10,... | collective-permute-start | bytes 884744 | tf_op jit(solution)/shard_map/ppermute | solution.py:291
  84.6 0.9 owned.1
  85.5 4.6 %collective-permute-done.1.second_ref = bf16[1152,128]{1,0:T(8,128)(2,1)S(1)} collective-permute-done((bf16[1152,128]{1,0:T(8,128)(2,1)S(1)}, bf16[1152,128]{1,0:T(8,128)(2,1)S(1)}, u32[]{:S(2)}, u32[]{:S(2)}) %collective-permute-start.1) | collective-permute-done | bytes 294944 | tf_op jit(solution)/shard_map/ppermute | solution.py:291
  90.2 2.8 %momentum.1 = (f32[72,4,1024]{2,1,0:T(4,128)}, f32[8,128]{1,0:T(8,128)S(1)}) custom-call(s32[72,128]{1,0:T(8,128)S(1)} %copy-done.1, f32[72,4,1024]{2,1,0:T(4,128)S(1)} %bitcast.10, bf16[576,128]{1,0:T(8,128)(2,1)S(1)} %get-tuple-element.16.total_ref.own_ref, bf16[576,128]{1,0:T(8,128)(2,1)S(1)} %collective-permute-done._.first_ref, ...), custom_call_target="tpu_custom_call" | custom-call | bytes 4000000 | tf_op jit(solution)/shard_map/momentum/pallas_call | solution.py:387
  92.9 4.8 %all-to-all-done.3 = bf16[128,8,128]{2,1,0:T(8,128)(2,1)S(1)} async-done(((bf16[128,8,128]{2,1,0:T(8,128)(2,1)}), bf16[128,8,128]{2,1,0:T(8,128)(2,1)S(1)}, u32[]{:S(2)}, u32[]{:S(2)}) %all-to-all-start.3) | async-done | bytes 262176 | tf_op jit(solution)/shard_map/all_to_all | solution.py:386
  97.7 0.6 select.1
  98.4 12.0 %all_to_all.41.pieces_ref = bf16[4,576,128]{2,1,0:T(8,128)(2,1)S(1)} all-to-all(bf16[4,576,128]{2,1,0:T(8,128)(2,1)S(1)} %select.1), channel_id=1, replica_groups=mesh['fsdp'=128,'rep'=4] {'rep'}, dimensions={0} | all-to-all | bytes 1179648 | tf_op jit(solution)/shard_map/all_to_all | solution.py:296
  110.4 0.9 update.1
Async XLA Ops:
  0.6 7.0 %copy-start = (f32[1,72,4,1024]{3,2,1,0:T(4,128)S(1)}, f32[1,72,4,1024]{3,2,1,0:T(4,128)}, u32[]{:S(2)}) copy-start(f32[1,72,4,1024]{3,2,1,0:T(4,128)} %param.5) | copy-start | bytes 3538948
  0.6 7.0 %copy-start.1 = (s32[72,128]{1,0:T(8,128)S(1)}, s32[72,128]{1,0:T(8,128)}, u32[]{:S(2)}) copy-start(s32[72,128]{1,0:T(8,128)} %lens_ref.3) | copy-start | bytes 110596
  0.7 7.0 %copy-start.2 = (s32[72]{0:T(128)S(1)}, s32[72]{0:T(128)}, u32[]{:S(2)}) copy-start(s32[72]{0:T(128)} %owner_ref.5) | copy-start | bytes 868
  2.8 12.1 %all-to-all-start = ((bf16[4,576,128]{2,1,0:T(8,128)(2,1)}), bf16[4,576,128]{2,1,0:T(8,128)(2,1)S(1)}, u32[]{:S(2)}, u32[]{:S(2)}) async-start(bf16[4,576,128]{2,1,0:T(8,128)(2,1)} %split.1), calls=%async_computation | async-start | bytes 1179648 | tf_op jit(solution)/shard_map/all_to_all | solution.py:296
  10.0 0.9 copy-start.3
  16.4 36.0 %all-to-all-start.1 = ((bf16[128,8,128]{2,1,0:T(8,128)(2,1)}), bf16[128,8,128]{2,1,0:T(8,128)(2,1)S(1)}, u32[]{:S(2)}, u32[]{:S(2)}) async-start(bf16[128,8,128]{2,1,0:T(8,128)(2,1)} %bitcast.2), calls=%async_computation.1 | async-start | bytes 524288 | tf_op jit(solution)/shard_map/all_to_all | solution.py:351
  37.2 7.4 %collective-permute-start = (bf16[576,128]{1,0:T(8,128)(2,1)S(1)}, bf16[576,128]{1,0:T(8,128)(2,1)S(1)}, u32[]{:S(2)}, u32[]{:S(2)}) collective-permute-start(bf16[576,128]{1,0:T(8,128)(2,1)S(1)} %get-tuple-element.16.total_ref.own_ref), channel_id=1, source_target_pairs={{0,1},{1,0},{2,3},{3,2},{4,7},{5,6},{6,5},{7,4},{8,9},{9,8},{10,11... | collective-permute-start | bytes 442376 | tf_op jit(solution)/shard_map/ppermute | solution.py:291
  52.8 14.6 %copy-start.4 = (bf16[1024,384]{1,0:T(8,128)(2,1)S(1)}, bf16[1024,384]{1,0:T(8,128)(2,1)}, u32[]{:S(2)}) copy-start(bf16[1024,384]{1,0:T(8,128)(2,1)} %copy-done.3) | copy-start | bytes 2359300
  75.9 21.8 %all-to-all-start.3 = ((bf16[128,8,128]{2,1,0:T(8,128)(2,1)}), bf16[128,8,128]{2,1,0:T(8,128)(2,1)S(1)}, u32[]{:S(2)}, u32[]{:S(2)}) async-start(bf16[128,8,128]{2,1,0:T(8,128)(2,1)} %bitcast.5), calls=%async_computation.3 | async-start | bytes 524288 | tf_op jit(solution)/shard_map/all_to_all | solution.py:386
  82.4 7.8 %collective-permute-start.1 = (bf16[1152,128]{1,0:T(8,128)(2,1)S(1)}, bf16[1152,128]{1,0:T(8,128)(2,1)S(1)}, u32[]{:S(2)}, u32[]{:S(2)}) collective-permute-start(bf16[1152,128]{1,0:T(8,128)(2,1)S(1)} %get-tuple-element.20._), channel_id=1, source_target_pairs={{0,3},{1,2},{2,1},{3,0},{4,5},{5,4},{6,7},{7,6},{8,11},{9,10},{10,... | collective-permute-start | bytes 884744 | tf_op jit(solution)/shard_map/ppermute | solution.py:291
